TPU v7x, 32 devices: a whole 2x2x4 slice. The times are simulated.
32 devices in a mesh: items: 16 (over z, y, core), blk: 2 (over x).
Axes of the slice: x: 2, y: 2, z: 4, core: 2. Of those that a mesh axis runs over, the one named last changes fastest.
Arguments:
- patches: bfloat16 [16, 1024, 768], P('items', 'blk'), may hold values from -6 to 6
- grid: int32 [16, 2], P('items'), may hold values from 8 to 128, as said below
- norm_attn: float32 [768], replicated, may hold values from 0.1 to 1.9
- w_query: bfloat16 [768, 768], P('items', 'blk'), may hold values from -0.0546875 to 0.0546875
- w_key: bfloat16 [768, 768], P('items', 'blk'), may hold values from -0.21875 to 0.21875
- w_value: bfloat16 [768, 768], P('items', 'blk'), may hold values from -0.21875 to 0.21875
- w_out: bfloat16 [768, 768], P('items', 'blk'), may hold values from -0.875 to 0.875
- norm_mlp: float32 [768], replicated, may hold values from 0.1 to 1.9
- w_gate: bfloat16 [768, 2048], P('items', 'blk'), may hold values from -0.21875 to 0.21875
- w_up: bfloat16 [768, 2048], P('items', 'blk'), may hold values from -0.21875 to 0.21875
- w_down: bfloat16 [2048, 768], P('items', 'blk'), may hold values from -0.125 to 0.125
- cotangent: bfloat16 [16, 1024, 768], P('items', 'blk'), may hold values from -6 to 6
Outputs:
- output: bfloat16 [16, 1024, 768], P('items', 'blk')
- grad_patches: bfloat16 [16, 1024, 768], P('items', 'blk')
- grad_norm_attn: float32 [768], replicated
- grad_w_query: float32 [768, 768], P('items', 'blk')
- grad_w_key: float32 [768, 768], P('items', 'blk')
- grad_w_value: float32 [768, 768], P('items', 'blk')
- grad_w_out: float32 [768, 768], P('items', 'blk')
- grad_norm_mlp: float32 [768], replicated
- grad_w_gate: float32 [768, 2048], P('items', 'blk')
- grad_w_up: float32 [768, 2048], P('items', 'blk')
- grad_w_down: float32 [2048, 768], P('items', 'blk')
Inputs may be any that keep to these rules, and one draw needn't show every extreme that they name: `grid`: for every plot height * width <= 1024 and 2 * height * width >= 1024; widths are (8) times 1, 2, 4 or 8; in every aligned group of 1 plots one has height * width = 1024.
All inputs are finite; a program needn't handle non-finite values.
Results may differ from a plain program's by a relative error of at most 0.02.
Values may be sent and summed in bfloat16 or wider, within the bound.
No kernel may reach another device: no remote copies, remote signals or barrier semaphores. Data moves between devices by JAX's collectives and lax.ppermute only.
A program may use at most 128 MiB of HBM per device.

v0:
```python
import jax
import jax.numpy as jnp
from jax import lax
from jax.sharding import PartitionSpec as P

HEAD = 64


EPSILON = 1e-06


def rms_norm(values, gain):
    return values * lax.rsqrt(jnp.mean(values * values, -1, keepdims=True) + EPSILON) * gain


def product(formula, left, right):
    return jnp.einsum(formula, left, right, preferred_element_type=jnp.float32)


def masked_scores(query_heads, key_part, first_key, counts):
    scores = product("iqhd,ikhd->ihqk", query_heads, key_part)
    places = first_key + jnp.arange(key_part.shape[1], dtype=jnp.int32)
    allowed = places[None, :] < counts[:, None]
    return jnp.where(allowed[:, None, None, :], scores, -1000000000.0)


def local(
    patches,
    grid,
    norm_attn,
    w_query,
    w_key,
    w_value,
    w_out,
    norm_mlp,
    w_gate,
    w_up,
    w_down,
    cotangent,
):
    columns = (
        lax.all_gather(w_query, "blk", axis=1, tiled=True),
        lax.all_gather(w_key, "blk", axis=1, tiled=True),
        lax.all_gather(w_value, "blk", axis=1, tiled=True),
        lax.all_gather(w_out, "blk", axis=1, tiled=True),
        lax.all_gather(w_gate, "blk", axis=1, tiled=True),
        lax.all_gather(w_up, "blk", axis=1, tiled=True),
        lax.all_gather(w_down, "blk", axis=1, tiled=True),
    )
    full_query, full_key, full_value, full_out, full_gate, full_up, full_down = (
        lax.all_gather(columns[0], "items", axis=0, tiled=True),
        lax.all_gather(columns[1], "items", axis=0, tiled=True),
        lax.all_gather(columns[2], "items", axis=0, tiled=True),
        lax.all_gather(columns[3], "items", axis=0, tiled=True),
        lax.all_gather(columns[4], "items", axis=0, tiled=True),
        lax.all_gather(columns[5], "items", axis=0, tiled=True),
        lax.all_gather(columns[6], "items", axis=0, tiled=True),
    )
    items_here, row_count, model_width = patches.shape
    head_count = model_width // HEAD
    blocks = lax.axis_size("blk")
    counts = grid[:, 0] * grid[:, 1]
    patch_rows = patches.astype(jnp.float32)
    normed = rms_norm(patch_rows, norm_attn).astype(jnp.bfloat16)
    queries = product("ird,de->ire", normed, full_query).astype(jnp.bfloat16)
    key_rows = product("ird,de->ire", normed, full_key).astype(jnp.bfloat16)
    value_rows = product("ird,de->ire", normed, full_value).astype(jnp.bfloat16)
    query_heads = queries.reshape(items_here, row_count, head_count, HEAD)

    def split_part(piece, shard_index):
        part_rows = lax.dynamic_slice_in_dim(piece, shard_index * row_count, row_count, 1)
        return part_rows.reshape(items_here, row_count, head_count, HEAD)

    stat_shape = (items_here, head_count, row_count)
    start_stats = (jnp.full(stat_shape, -1e30, jnp.float32), jnp.zeros(stat_shape, jnp.float32))
    carried = start_stats
    key_piece = lax.all_gather(key_rows, "blk", axis=1, tiled=True)
    shards = key_piece.shape[1] // row_count

    def stats_one_shard(running, shard_index):
        running_max, running_sum = running
        key_part = split_part(key_piece, shard_index)
        scores = masked_scores(query_heads, key_part, shard_index * row_count, counts)
        new_max = jnp.maximum(running_max, jnp.max(scores, -1))
        new_sum = running_sum * jnp.exp(running_max - new_max) + jnp.sum(
            jnp.exp(scores - new_max[..., None]), -1
        )
        return ((new_max, new_sum), None)

    carried, unused = lax.scan(stats_one_shard, carried, jnp.arange(shards, dtype=jnp.int32))
    totals = carried
    log_total = totals[0] + jnp.log(totals[1])
    start_values = jnp.zeros((items_here, head_count, row_count, HEAD), jnp.float32)
    carried = start_values
    values_key_piece = lax.all_gather(key_rows, "blk", axis=1, tiled=True)
    value_piece = lax.all_gather(value_rows, "blk", axis=1, tiled=True)
    shards = values_key_piece.shape[1] // row_count

    def values_one_shard(accumulated, shard_index):
        key_part = split_part(values_key_piece, shard_index)
        value_part = split_part(value_piece, shard_index)
        scores = masked_scores(query_heads, key_part, shard_index * row_count, counts)
        weights_low = jnp.exp(scores - log_total[..., None]).astype(jnp.bfloat16)
        return (accumulated + product("ihqk,ikhd->ihqd", weights_low, value_part), None)

    carried, unused = lax.scan(values_one_shard, carried, jnp.arange(shards, dtype=jnp.int32))
    attended = carried.transpose(0, 2, 1, 3).reshape(items_here, row_count, model_width)
    attended_low = attended.astype(jnp.bfloat16)
    middle = patch_rows + product("ird,de->ire", attended_low, full_out)
    normed_mlp = rms_norm(middle, norm_mlp).astype(jnp.bfloat16)
    gate_in = product("ird,df->irf", normed_mlp, full_gate)
    upward = product("ird,df->irf", normed_mlp, full_up)
    activated = jax.nn.gelu(gate_in, approximate=True)
    hidden = (activated * upward).astype(jnp.bfloat16)
    output = (middle + product("irf,fd->ird", hidden, full_down)).astype(jnp.bfloat16)
    grad_down = product("irf,ird->fd", hidden, cotangent)
    grad_hidden = product("ird,fd->irf", cotangent, full_down)
    unused_gelu, gelu_back = jax.vjp(lambda inner: jax.nn.gelu(inner, approximate=True), gate_in)
    grad_gate_in = gelu_back(grad_hidden * upward)[0].astype(jnp.bfloat16)
    grad_upward = (grad_hidden * activated).astype(jnp.bfloat16)
    grad_gate = product("ird,irf->df", normed_mlp, grad_gate_in)
    grad_up = product("ird,irf->df", normed_mlp, grad_upward)
    grad_normed_mlp = product("irf,df->ird", grad_gate_in, full_gate) + product(
        "irf,df->ird", grad_upward, full_up
    )
    unused_norm, second_back = jax.vjp(rms_norm, middle, norm_mlp)
    grad_middle_part, grad_norm_mlp = second_back(grad_normed_mlp)
    grad_middle = cotangent.astype(jnp.float32) + grad_middle_part
    branch_grad = grad_middle.astype(jnp.bfloat16)
    grad_out = product("ird,ire->de", attended_low, branch_grad)
    grad_attended = product("ire,de->ird", branch_grad, full_out).astype(jnp.bfloat16)
    grad_heads = grad_attended.reshape(items_here, row_count, head_count, HEAD)
    delta = jnp.einsum(
        "iqhd,iqhd->ihq",
        grad_heads.astype(jnp.float32),
        attended.reshape(items_here, row_count, head_count, HEAD),
    )
    gathered_keys, gathered_values = (
        lax.all_gather(key_rows, "blk", axis=1, tiled=True),
        lax.all_gather(value_rows, "blk", axis=1, tiled=True),
    )
    query_start = jnp.zeros((items_here, row_count, head_count, HEAD), jnp.float32)

    def back_shard(grad_query, shard_index):
        key_part = split_part(gathered_keys, shard_index)
        value_part = split_part(gathered_values, shard_index)
        scores = masked_scores(query_heads, key_part, shard_index * row_count, counts)
        chances = jnp.exp(scores - log_total[..., None])
        grad_chances = product("iqhd,ikhd->ihqk", grad_heads, value_part)
        grad_scores = (chances * (grad_chances - delta[..., None])).astype(jnp.bfloat16)
        grad_query = grad_query + product("ihqk,ikhd->iqhd", grad_scores, key_part)
        key_term = product("ihqk,iqhd->ikhd", grad_scores, query_heads)
        value_term = product("ihqk,iqhd->ikhd", chances.astype(jnp.bfloat16), grad_heads)
        return (
            grad_query,
            (
                key_term.reshape(items_here, row_count, model_width),
                value_term.reshape(items_here, row_count, model_width),
            ),
        )

    grad_query, key_value_terms = lax.scan(
        back_shard, query_start, jnp.arange(blocks, dtype=jnp.int32)
    )
    key_sum, value_sum = (
        lax.psum_scatter(
            key_value_terms[0].astype(jnp.bfloat16), "blk", scatter_dimension=0, tiled=True
        ).astype(jnp.float32),
        lax.psum_scatter(
            key_value_terms[1].astype(jnp.bfloat16), "blk", scatter_dimension=0, tiled=True
        ).astype(jnp.float32),
    )
    grad_keys = key_sum[0].astype(jnp.bfloat16)
    grad_values = value_sum[0].astype(jnp.bfloat16)
    grad_queries = grad_query.reshape(items_here, row_count, model_width).astype(jnp.bfloat16)
    grad_wq = product("ird,ire->de", normed, grad_queries)
    grad_wk = product("ird,ire->de", normed, grad_keys)
    grad_wv = product("ird,ire->de", normed, grad_values)
    grad_normed = (
        product("ire,de->ird", grad_queries, full_query)
        + product("ire,de->ird", grad_keys, full_key)
        + product("ire,de->ird", grad_values, full_value)
    )
    unused_first, first_back = jax.vjp(rms_norm, patch_rows, norm_attn)
    grad_rows_part, grad_norm_attn = first_back(grad_normed)
    grad_patches = (grad_middle + grad_rows_part).astype(jnp.bfloat16)
    gain_total = lax.psum((grad_norm_attn, grad_norm_mlp), ("items", "blk"))
    by_rows = (
        lax.psum_scatter(
            grad_wq.astype(jnp.bfloat16), "items", scatter_dimension=0, tiled=True
        ).astype(jnp.float32),
        lax.psum_scatter(
            grad_wk.astype(jnp.bfloat16), "items", scatter_dimension=0, tiled=True
        ).astype(jnp.float32),
        lax.psum_scatter(
            grad_wv.astype(jnp.bfloat16), "items", scatter_dimension=0, tiled=True
        ).astype(jnp.float32),
        lax.psum_scatter(
            grad_out.astype(jnp.bfloat16), "items", scatter_dimension=0, tiled=True
        ).astype(jnp.float32),
        lax.psum_scatter(
            grad_gate.astype(jnp.bfloat16), "items", scatter_dimension=0, tiled=True
        ).astype(jnp.float32),
        lax.psum_scatter(
            grad_up.astype(jnp.bfloat16), "items", scatter_dimension=0, tiled=True
        ).astype(jnp.float32),
        lax.psum_scatter(
            grad_down.astype(jnp.bfloat16), "items", scatter_dimension=0, tiled=True
        ).astype(jnp.float32),
    )
    final_shards = (
        lax.psum_scatter(
            by_rows[0].astype(jnp.bfloat16), "blk", scatter_dimension=1, tiled=True
        ).astype(jnp.float32),
        lax.psum_scatter(
            by_rows[1].astype(jnp.bfloat16), "blk", scatter_dimension=1, tiled=True
        ).astype(jnp.float32),
        lax.psum_scatter(
            by_rows[2].astype(jnp.bfloat16), "blk", scatter_dimension=1, tiled=True
        ).astype(jnp.float32),
        lax.psum_scatter(
            by_rows[3].astype(jnp.bfloat16), "blk", scatter_dimension=1, tiled=True
        ).astype(jnp.float32),
        lax.psum_scatter(
            by_rows[4].astype(jnp.bfloat16), "blk", scatter_dimension=1, tiled=True
        ).astype(jnp.float32),
        lax.psum_scatter(
            by_rows[5].astype(jnp.bfloat16), "blk", scatter_dimension=1, tiled=True
        ).astype(jnp.float32),
        lax.psum_scatter(
            by_rows[6].astype(jnp.bfloat16), "blk", scatter_dimension=1, tiled=True
        ).astype(jnp.float32),
    )
    return (
        output,
        grad_patches,
        gain_total[0],
        final_shards[0],
        final_shards[1],
        final_shards[2],
        final_shards[3],
        gain_total[1],
        final_shards[4],
        final_shards[5],
        final_shards[6],
    )


def solution(mesh):
    placed = (
        P("items", "blk", None),
        P("items", None),
        P(),
        P("items", "blk"),
        P("items", "blk"),
        P("items", "blk"),
        P("items", "blk"),
        P(),
        P("items", "blk"),
        P("items", "blk"),
        P("items", "blk"),
        P("items", "blk", None),
    )
    return jax.shard_map(
        local,
        mesh=mesh,
        in_specs=placed,
        out_specs=(
            P("items", "blk", None),
            P("items", "blk", None),
            P(),
            P("items", "blk"),
            P("items", "blk"),
            P("items", "blk"),
            P("items", "blk"),
            P(),
            P("items", "blk"),
            P("items", "blk"),
            P("items", "blk"),
        ),
        check_vma=False,
    )
```

profile of v0, /device:TPU:0, one launch (start us, length us, event | category | flops | bytes accessed | tf_op | source)
XLA Modules:
  0.0 1038.9 jit_solution(7763867605922915732)
XLA Ops:
  7.2 7.2 all_gather.51
  14.5 5.0 all_gather.56
  19.5 5.6 all_gather.54
  27.2 26.1 %all-gather.12.cloned.1.call-done = bf16[768,768]{1,0:T(8,128)(2,1)} async-done(((bf16[48,768]{1,0:T(8,128)(2,1)}), bf16[768,768]{1,0:T(8,128)(2,1)}) %all-gather.12.cloned.1.call-update) | async-done | bytes 1179664 | tf_op jit(solution)/shard_map/all_gather | solution.py:52
  53.4 3.2 convolution_convert_fusion.10
  56.7 36.3 %all-gather.16.cloned.1.call-done = bf16[768,768]{1,0:T(8,128)(2,1)} async-done(((bf16[48,768]{1,0:T(8,128)(2,1)}), bf16[768,768]{1,0:T(8,128)(2,1)}) %all-gather.16.cloned.1.call-update) | async-done | bytes 1179664 | tf_op jit(solution)/shard_map/all_gather | solution.py:53
  93.0 3.0 convolution_convert_fusion.8
  96.1 4.7 all_gather.59
  100.9 5.4 all_gather.63
  106.4 5.4 all_gather.61
  111.9 5.4 all_gather.65
  119.5 13.1 %all-gather.14.cloned.1.call-done = bf16[768,768]{1,0:T(8,128)(2,1)} async-done(((bf16[48,768]{1,0:T(8,128)(2,1)}), bf16[768,768]{1,0:T(8,128)(2,1)}) %all-gather.14.cloned.1.call-update) | async-done | bytes 1179664 | tf_op jit(solution)/shard_map/all_gather | solution.py:51
  135.0 25.8 %all-gather.26.cloned.1.call-done = bf16[1024,768]{1,0:T(8,128)(2,1)} async-done(((bf16[512,768]{1,0:T(8,128)(2,1)}), bf16[1024,768]{1,0:T(8,128)(2,1)}) %all-gather.26.cloned.1.call-update) | async-done | bytes 1572880 | tf_op jit(solution)/shard_map/all_gather | solution.py:95
  160.8 2.6 copy.41
  163.4 15.0 %while.39 = (s32[]{:T(128)}, f32[1,12,512]{2,1,0:T(8,128)S(1)}, f32[1,12,512]{2,1,0:T(8,128)S(1)}, s32[2]{0:T(128)S(1)}, s32[1]{0:T(128)}, /*index=5*/bf16[1,102...) while((s32[]{:T(128)}, f32[1,12,512]{2,1,0:T(8,128)S(1)}, ...), condition=%wide.region_4.5_spmd.clone, body=%wide.region_1.4_spmd.clone.sunk | while | flops 418413568 | bytes 28632772 | solution.py:90
  165.8 2.8 bitcast_reduce_fusion.2
  173.4 2.8 bitcast_reduce_fusion.2
  178.4 11.6 %all-gather.28.cloned.1.call-done = bf16[1024,768]{1,0:T(8,128)(2,1)} async-done(((bf16[512,768]{1,0:T(8,128)(2,1)}), bf16[1024,768]{1,0:T(8,128)(2,1)}) %all-gather.28.cloned.1.call-update) | async-done | bytes 1572880 | tf_op jit(solution)/shard_map/all_gather | solution.py:96
  190.0 2.6 copy.42
  192.6 17.8 %while.40 = (s32[]{:T(128)}, f32[1,12,512,64]{2,3,1,0:T(8,128)}, s32[2]{0:T(128)S(1)}, s32[1]{0:T(128)}, bf16[1,1024,768]{1,2,0:T(8,128)(2,1)}, /*index=5*/bf16[...) while((s32[]{:T(128)}, f32[1,12,512,64]{2,3,1,0:T(8,128)}, ...), condition=%wide.region_6.7_spmd.clone, body=%wide.region_5.6_spmd.clone.sunk | while | flops 815531008 | bytes 8676557 | solution.py:106
  195.4 5.3 bitcast_add_fusion.8
  203.5 6.7 bitcast_add_fusion.8
  212.1 18.5 %all-gather.18.cloned.1.call-done = bf16[768,768]{1,0:T(8,128)(2,1)} async-done(((bf16[48,768]{1,0:T(8,128)(2,1)}), bf16[768,768]{1,0:T(8,128)(2,1)}) %all-gather.18.cloned.1.call-update) | async-done | bytes 1179664 | tf_op jit(solution)/shard_map/all_gather | solution.py:54
  230.5 2.2 multiply_reduce_fusion
  234.2 42.8 %all-gather.22.cloned.1.call-done = bf16[768,2048]{1,0:T(8,128)(2,1)} async-done(((bf16[48,2048]{1,0:T(8,128)(2,1)}), bf16[768,2048]{1,0:T(8,128)(2,1)}) %all-gather.22.cloned.1.call-update) | async-done | bytes 3145744 | tf_op jit(solution)/shard_map/all_gather | solution.py:56
  277.0 5.6 fusion.70
  282.7 40.7 %all-gather.20.cloned.1.call-done = bf16[768,2048]{1,0:T(8,128)(2,1)} async-done(((bf16[48,2048]{1,0:T(8,128)(2,1)}), bf16[768,2048]{1,0:T(8,128)(2,1)}) %all-gather.20.cloned.1.call-update) | async-done | bytes 3145744 | tf_op jit(solution)/shard_map/all_gather | solution.py:55
  323.3 5.7 fusion.69
  329.0 40.6 %all-gather.24.cloned.1.call-done = bf16[2048,768]{1,0:T(8,128)(2,1)} async-done(((bf16[128,768]{1,0:T(8,128)(2,1)}), bf16[2048,768]{1,0:T(8,128)(2,1)}) %all-gather.24.cloned.1.call-update) | async-done | bytes 3145744 | tf_op jit(solution)/shard_map/all_gather | solution.py:57
  369.7 8.7 multiply_convert_fusion.1
  388.8 45.0 %while.41 = (s32[]{:T(128)}, f32[1,512,12,64]{1,3,2,0:T(8,128)}, bf16[2,1,512,768]{2,3,1,0:T(8,128)(2,1)}, bf16[2,1,512,768]{2,3,1,0:T(8,128)(2,1)}, s32[2]{0:T(...) while((s32[]{:T(128)}, f32[1,512,12,64]{1,3,2,0:T(8,128)}, ...), condition=%wide.region_10.11_spmd.clone, body=%wide.region_9.10_spmd.clone.sunk | while | flops 2039219200 | bytes 114108384 | solution.py:162
  390.7 2.2 constant_dynamic-slice_fusion.12
  394.8 4.6 fusion.143
  399.4 5.2 multiply_convert_fusion.5
  404.6 2.2 bitcast_add_fusion.9
  412.2 2.2 constant_dynamic-slice_fusion.12
  416.3 4.6 fusion.143
  421.0 5.2 multiply_convert_fusion.5
  426.2 3.7 bitcast_add_fusion.9
  435.3 3.0 convolution_convert_fusion.3
  442.0 16.9 %reduce-scatter.27.cloned.1.call-done = bf16[1,1,512,768]{2,3,1,0:T(8,128)(2,1)} async-done(((bf16[2,1,512,768]{2,3,1,0:T(8,128)(2,1)}), bf16[1,1,512,768]{2,3,1,0:T(8,128)(2,1)}) %reduce-scatter.27.cloned.1.call-update) | async-done | bytes 786448 | tf_op jit(solution)/shard_map/reduce_scatter | solution.py:166
  458.9 3.1 convolution_convert_fusion.5
  462.3 25.1 %reduce-scatter.29.cloned.1.call-done = bf16[1,1,512,768]{2,3,1,0:T(8,128)(2,1)} async-done(((bf16[2,1,512,768]{2,3,1,0:T(8,128)(2,1)}), bf16[1,1,512,768]{2,3,1,0:T(8,128)(2,1)}) %reduce-scatter.29.cloned.1.call-update) | async-done | bytes 786448 | tf_op jit(solution)/shard_map/reduce_scatter | solution.py:169
  487.4 3.2 convolution_convert_fusion.4
  490.6 5.2 convolution_convert_fusion
  495.9 53.0 %reduce-scatter.37.cloned.1.call-done = bf16[48,768]{1,0:T(8,128)(2,1)} async-done(((bf16[768,768]{1,0:T(8,128)(2,1)}), bf16[48,768]{1,0:T(8,128)(2,1)}) %reduce-scatter.37.cloned.1.call-update) | async-done | bytes 73744 | tf_op jit(solution)/shard_map/reduce_scatter | solution.py:198
  550.7 58.9 %reduce-scatter.31.cloned.1.call-done = bf16[48,768]{1,0:T(8,128)(2,1)} async-done(((bf16[768,768]{1,0:T(8,128)(2,1)}), bf16[48,768]{1,0:T(8,128)(2,1)}) %reduce-scatter.31.cloned.1.call-update) | async-done | bytes 73744 | tf_op jit(solution)/shard_map/reduce_scatter | solution.py:189
  611.4 5.1 convolution_convert_fusion.1
  616.5 5.2 convolution_convert_fusion.2
  621.8 48.4 %reduce-scatter.33.cloned.1.call-done = bf16[48,768]{1,0:T(8,128)(2,1)} async-done(((bf16[768,768]{1,0:T(8,128)(2,1)}), bf16[48,768]{1,0:T(8,128)(2,1)}) %reduce-scatter.33.cloned.1.call-update) | async-done | bytes 73744 | tf_op jit(solution)/shard_map/reduce_scatter | solution.py:192
  671.9 58.8 %reduce-scatter.35.cloned.1.call-done = bf16[48,768]{1,0:T(8,128)(2,1)} async-done(((bf16[768,768]{1,0:T(8,128)(2,1)}), bf16[48,768]{1,0:T(8,128)(2,1)}) %reduce-scatter.35.cloned.1.call-update) | async-done | bytes 73744 | tf_op jit(solution)/shard_map/reduce_scatter | solution.py:195
  732.5 5.7 fusion.45
  738.2 61.5 %reduce-scatter.47.cloned.1.call-done = bf16[128,768]{1,0:T(8,128)(2,1)} async-done(((bf16[2048,768]{1,0:T(8,128)(2,1)}), bf16[128,768]{1,0:T(8,128)(2,1)}) %reduce-scatter.47.cloned.1.call-update) | async-done | bytes 196624 | tf_op jit(solution)/shard_map/reduce_scatter | solution.py:207
  801.5 3.3 fusion.72
  804.8 6.8 reduce-scatter.55.cloned.1.call-done
  813.2 12.0 %reduce-scatter.49.cloned.1.call-done = bf16[384,48]{1,0:T(8,128)(2,1)} async-done(((bf16[768,48]{1,0:T(8,128)(2,1)}), bf16[384,48]{1,0:T(8,128)(2,1)}) %reduce-scatter.49.cloned.1.call-update) | async-done | bytes 36880
  826.9 3.6 fusion.51
  830.4 64.9 %reduce-scatter.43.cloned.1.call-done = bf16[48,2048]{1,0:T(8,128)(2,1)} async-done(((bf16[768,2048]{1,0:T(8,128)(2,1)}), bf16[48,2048]{1,0:T(8,128)(2,1)}) %reduce-scatter.43.cloned.1.call-update) | async-done | bytes 196624 | tf_op jit(solution)/shard_map/reduce_scatter | solution.py:204
  895.5 4.5 fusion.36
  900.0 64.3 %reduce-scatter.39.cloned.1.call-done = bf16[48,2048]{1,0:T(8,128)(2,1)} async-done(((bf16[768,2048]{1,0:T(8,128)(2,1)}), bf16[48,2048]{1,0:T(8,128)(2,1)}) %reduce-scatter.39.cloned.1.call-update) | async-done | bytes 196624 | tf_op jit(solution)/shard_map/reduce_scatter | solution.py:201
  964.3 39.8 %all-reduce = (f32[768]{0:T(1024)}, f32[768]{0:T(1024)}) all-reduce(f32[768]{0:T(1024)S(1)} %get-tuple-element.334, f32[768]{0:T(1024)S(1)} %get-tuple-element.332), channel_id=1, replica_groups=mesh['items'=16,'blk'=2] {'items','blk'}, use_global_device_ids=true, to_apply=%region_15.16 | all-reduce | flops 1536 | bytes 12288 | tf_op jit(solution)/shard_map/psum | solution.py:187
  1004.2 2.7 fusion.39
  1011.9 5.6 reduce-scatter.45.cloned.1.call-done
  1019.0 11.6 %reduce-scatter.41.cloned.1.call-done = bf16[48,1024]{1,0:T(8,128)(2,1)} async-done(((bf16[48,2048]{1,0:T(8,128)(2,1)}), bf16[48,1024]{1,0:T(8,128)(2,1)}) %reduce-scatter.41.cloned.1.call-update) | async-done | bytes 98320 | tf_op jit(solution)/shard_map/reduce_scatter | solution.py:224
  (230 shorter events, 70.3 us)
Async XLA Ops:
  7.2 46.2 %all-gather.12.cloned.1.call-start = ((), (), s32[]{:S(2)}) async-start(), calls=%async_computation.16 | async-start | bytes 1253376 | tf_op jit(solution)/shard_map/all_gather | solution.py:52
  14.5 78.5 %all-gather.16.cloned.1.call-start = ((), (), s32[]{:S(2)}) async-start(), calls=%async_computation.18 | async-start | bytes 1253376 | tf_op jit(solution)/shard_map/all_gather | solution.py:53
  19.5 113.1 %all-gather.14.cloned.1.call-start = ((), (), s32[]{:S(2)}) async-start(), calls=%async_computation.17 | async-start | bytes 1253376 | tf_op jit(solution)/shard_map/all_gather | solution.py:51
  25.2 135.6 %all-gather.26.cloned.1.call-start = ((), (), s32[]{:S(2)}) async-start(), calls=%async_computation.34 | async-start | bytes 2359296 | tf_op jit(solution)/shard_map/all_gather | solution.py:95
  27.2 105.4 %copy-start.31 = (f32[512]{0:T(512)}, f32[512]{0:T(512)S(1)}, u32[]{:S(2)}) copy-start(f32[512]{0:T(512)S(1)} %fusion.60) | copy-start | bytes 6148
  27.2 65.8 %copy-start.7 = (bf16[1,512,768]{2,1,0:T(8,128)(2,1)S(1)}, bf16[1,512,768]{2,1,0:T(8,128)(2,1)}, u32[]{:S(2)}) copy-start(bf16[1,512,768]{2,1,0:T(8,128)(2,1)} %param.18) | copy-start | bytes 2359300
  27.2 65.8 %copy-start.33 = (f32[768]{0:T(1024)S(1)}, f32[768]{0:T(1024)}, u32[]{:S(2)}) copy-start(f32[768]{0:T(1024)} %param.20) | copy-start | bytes 9220
  56.6 39.4 %copy-start.28 = (bf16[48,384]{1,0:T(8,128)(2,1)S(1)}, bf16[48,384]{1,0:T(8,128)(2,1)}, u32[]{:S(2)}) copy-start(bf16[48,384]{1,0:T(8,128)(2,1)} %param.24) | copy-start | bytes 110596
  56.6 44.2 %copy-start.25 = (bf16[48,1024]{1,0:T(8,128)(2,1)S(1)}, bf16[48,1024]{1,0:T(8,128)(2,1)}, u32[]{:S(2)}) copy-start(bf16[48,1024]{1,0:T(8,128)(2,1)} %param.27) | copy-start | bytes 294916
  56.7 49.7 %copy-start.26 = (bf16[48,1024]{1,0:T(8,128)(2,1)S(1)}, bf16[48,1024]{1,0:T(8,128)(2,1)}, u32[]{:S(2)}) copy-start(bf16[48,1024]{1,0:T(8,128)(2,1)} %param.26) | copy-start | bytes 294916
  56.7 133.3 %all-gather.28.cloned.1.call-start = ((), (), s32[]{:S(2)}) async-start(), calls=%async_computation.35 | async-start | bytes 2359296 | tf_op jit(solution)/shard_map/all_gather | solution.py:96
  96.0 15.9 %copy-start.27 = (bf16[128,384]{1,0:T(8,128)(2,1)S(1)}, bf16[128,384]{1,0:T(8,128)(2,1)}, u32[]{:S(2)}) copy-start(bf16[128,384]{1,0:T(8,128)(2,1)} %param.28) | copy-start | bytes 294916
  96.0 21.6 %copy-start.36 = (s32[1,2]{1,0:T(1,128)S(1)}, s32[1,2]{1,0:T(1,128)}, u32[]{:S(2)}) copy-start(s32[1,2]{1,0:T(1,128)} %param.19) | copy-start | bytes 28
  96.0 134.5 %all-gather.18.cloned.1.call-start = ((), (), s32[]{:S(2)}) async-start(), calls=%async_computation.19 | async-start | bytes 1253376 | tf_op jit(solution)/shard_map/all_gather | solution.py:54
  100.8 176.2 %all-gather.22.cloned.1.call-start = ((), (), s32[]{:S(2)}) async-start(), calls=%async_computation.21 | async-start | bytes 3342336 | tf_op jit(solution)/shard_map/all_gather | solution.py:56
  106.3 217.0 %all-gather.20.cloned.1.call-start = ((), (), s32[]{:S(2)}) async-start(), calls=%async_computation.20 | async-start | bytes 3342336 | tf_op jit(solution)/shard_map/all_gather | solution.py:55
  111.8 257.9 %all-gather.24.cloned.1.call-start = ((), (), s32[]{:S(2)}) async-start(), calls=%async_computation.22 | async-start | bytes 3342336 | tf_op jit(solution)/shard_map/all_gather | solution.py:57
  117.3 341.6 %reduce-scatter.27.cloned.1.call-start = ((), (), s32[]{:S(2)}) async-start(), calls=%async_computation.23 | async-start | bytes 2359296 | tf_op jit(solution)/shard_map/reduce_scatter | solution.py:166
  210.4 20.1 %copy-start.8 = (bf16[1,512,768]{2,1,0:T(8,128)(2,1)S(1)}, bf16[1,512,768]{2,1,0:T(8,128)(2,1)}, u32[]{:S(2)}) copy-start(bf16[1,512,768]{2,1,0:T(8,128)(2,1)} %param.18) | copy-start | bytes 2359300
  212.1 20.7 %copy-start.13 = (bf16[1,512,12,64]{1,3,2,0:T(8,128)(2,1)}, bf16[1,512,12,64]{1,3,2,0:T(8,128)(2,1)S(1)}, u32[]{:S(2)}) copy-start(bf16[1,512,12,64]{1,3,2,0:T(8,128)(2,1)S(1)} %bitcast_convert_fusion) | copy-start | bytes 2359300
  230.5 3.5 copy-start.35
  234.2 89.1 %copy-start.18 = (bf16[512,768]{1,0:T(8,128)(2,1)}, bf16[512,768]{1,0:T(8,128)(2,1)S(1)}, u32[]{:S(2)}) copy-start(bf16[512,768]{1,0:T(8,128)(2,1)S(1)} %fusion.46) | copy-start | bytes 2359300
  282.6 87.0 %copy-start.22 = (bf16[1,512,768]{2,1,0:T(8,128)(2,1)S(1)}, bf16[1,512,768]{2,1,0:T(8,128)(2,1)}, u32[]{:S(2)}) copy-start(bf16[1,512,768]{2,1,0:T(8,128)(2,1)} %param.29) | copy-start | bytes 2359300
  369.7 8.7 copy-start.38
  378.3 1.9 copy-start.41
  378.3 2.1 copy-start.40
  378.4 2.6 copy-start.12
  378.4 3.9 copy-start.37
  389.3 3.6 copy-start.2
  390.6 2.2 copy-start
  406.9 2.0 copy-start.4
  406.9 2.0 copy-start.14
  406.9 2.1 copy-start.16
  409.0 1.9 copy-start.3
  409.2 1.7 copy-start.17
  410.9 3.6 copy-start.2
  412.2 2.2 copy-start
  429.8 2.0 copy-start.4
  429.8 2.0 copy-start.14
  429.8 2.1 copy-start.16
  431.9 1.9 copy-start.3
  432.1 1.7 copy-start.17
  433.9 53.5 %reduce-scatter.29.cloned.1.call-start = ((), (), s32[]{:S(2)}) async-start(), calls=%async_computation.24 | async-start | bytes 2359296 | tf_op jit(solution)/shard_map/reduce_scatter | solution.py:169
  434.6 3.7 copy-start.1
  434.6 114.3 %reduce-scatter.37.cloned.1.call-start = ((), (), s32[]{:S(2)}) async-start(), calls=%async_computation.28 | async-start | bytes 1253376 | tf_op jit(solution)/shard_map/reduce_scatter | solution.py:198
  438.2 171.3 %reduce-scatter.31.cloned.1.call-start = ((), (), s32[]{:S(2)}) async-start(), calls=%async_computation.25 | async-start | bytes 1253376 | tf_op jit(solution)/shard_map/reduce_scatter | solution.py:189
  439.8 19.1 %copy-start.10 = (bf16[1,512,768]{2,1,0:T(8,128)(2,1)S(1)}, bf16[1,512,768]{2,1,0:T(8,128)(2,1)}, u32[]{:S(2)}) copy-start(bf16[1,512,768]{2,1,0:T(8,128)(2,1)} %param.18) | copy-start | bytes 2359300
  441.9 228.2 %reduce-scatter.33.cloned.1.call-start = ((), (), s32[]{:S(2)}) async-start(), calls=%async_computation.26 | async-start | bytes 1253376 | tf_op jit(solution)/shard_map/reduce_scatter | solution.py:192
  462.0 28.6 %copy-start.23 = (bf16[1,512,768]{2,1,0:T(8,128)(2,1)S(1)}, bf16[1,512,768]{2,1,0:T(8,128)(2,1)}, u32[]{:S(2)}) copy-start(bf16[1,512,768]{2,1,0:T(8,128)(2,1)} %param.29) | copy-start | bytes 2359300
  462.1 268.7 %reduce-scatter.35.cloned.1.call-start = ((), (), s32[]{:S(2)}) async-start(), calls=%async_computation.27 | async-start | bytes 1253376 | tf_op jit(solution)/shard_map/reduce_scatter | solution.py:195
  490.6 309.1 %reduce-scatter.47.cloned.1.call-start = ((), (), s32[]{:S(2)}) async-start(), calls=%async_computation.33 | async-start | bytes 3342336 | tf_op jit(solution)/shard_map/reduce_scatter | solution.py:207
  495.8 115.5 %copy-start.19 = (bf16[512,768]{1,0:T(8,128)(2,1)S(1)}, bf16[512,768]{1,0:T(8,128)(2,1)}, u32[]{:S(2)}) copy-start(bf16[512,768]{1,0:T(8,128)(2,1)} %copy-done.18) | copy-start | bytes 2359300
  495.8 315.8 %reduce-scatter.55.cloned.1.call-start = ((), (), s32[]{:S(2)}) async-start(), calls=%async_computation.39 | async-start | bytes 294912
  550.6 274.6 %reduce-scatter.49.cloned.1.call-start = ((), (), s32[]{:S(2)}) async-start(), calls=%async_computation.36 | async-start | bytes 294912
  611.3 284.1 %reduce-scatter.43.cloned.1.call-start = ((), (), s32[]{:S(2)}) async-start(), calls=%async_computation.31 | async-start | bytes 3342336 | tf_op jit(solution)/shard_map/reduce_scatter | solution.py:204
  616.5 347.8 %reduce-scatter.39.cloned.1.call-start = ((), (), s32[]{:S(2)}) async-start(), calls=%async_computation.29 | async-start | bytes 3342336 | tf_op jit(solution)/shard_map/reduce_scatter | solution.py:201
  621.7 385.2 %reduce-scatter.51.cloned.1.call-start = ((), (), s32[]{:S(2)}) async-start(), calls=%async_computation.37 | async-start | bytes 294912
  671.9 336.7 %reduce-scatter.53.cloned.1.call-start = ((), (), s32[]{:S(2)}) async-start(), calls=%async_computation.38 | async-start | bytes 294912
  732.4 69.1 %copy-start.21 = (bf16[1,512,12,64]{1,3,2,0:T(8,128)(2,1)S(1)}, bf16[1,512,12,64]{1,3,2,0:T(8,128)(2,1)}, u32[]{:S(2)}) copy-start(bf16[1,512,12,64]{1,3,2,0:T(8,128)(2,1)} %copy-done.20) | copy-start | bytes 2359300
  732.5 277.7 %reduce-scatter.57.cloned.1.call-start = ((), (), s32[]{:S(2)}) async-start(), calls=%async_computation.40 | async-start | bytes 294912
  801.4 216.0 %reduce-scatter.45.cloned.1.call-start = ((), (), s32[]{:S(2)}) async-start(), calls=%async_computation.32 | async-start | bytes 294912 | tf_op jit(solution)/shard_map/reduce_scatter | solution.py:227
  826.9 68.6 %copy-start.24 = (bf16[1,1,512,768]{2,3,1,0:T(8,128)(2,1)S(1)}, bf16[1,1,512,768]{2,3,1,0:T(8,128)(2,1)}, u32[]{:S(2)}) copy-start(bf16[1,1,512,768]{2,3,1,0:T(8,128)(2,1)} %reduce-scatter.29.cloned.1.call-done) | copy-start | bytes 2359300
  895.4 68.9 %copy-start.30 = (f32[512]{0:T(512)S(1)}, f32[512]{0:T(512)}, u32[]{:S(2)}) copy-start(f32[512]{0:T(512)} %copy-done.29) | copy-start | bytes 6148
  895.4 135.2 %reduce-scatter.41.cloned.1.call-start = ((), (), s32[]{:S(2)}) async-start(), calls=%async_computation.30 | async-start | bytes 294912 | tf_op jit(solution)/shard_map/reduce_scatter | solution.py:224
  (11 other events, 13.1 us)
Sparse Core Ops, SparseCore 0:
  14.6 38.7 all-gather.11
  55.6 37.3 all-gather.15
  95.3 37.2 all-gather.13
  134.6 26.1 all-gather.25
  162.8 27.1 all-gather.27
  192.2 38.3 all-gather.17
  232.8 44.1 all-gather.21
  279.3 43.9 all-gather.19
  325.6 43.9 all-gather.23
  434.0 24.8 reduce-scatter.26
  461.2 26.0 reduce-scatter.28
  490.8 58.0 reduce-scatter.36
  552.5 57.0 reduce-scatter.30
  613.1 57.0 reduce-scatter.32
  673.6 57.0 reduce-scatter.34
  734.4 65.2 reduce-scatter.46
  801.8 9.7 reduce-scatter.54
  814.3 10.9 reduce-scatter.48
  829.1 66.2 reduce-scatter.42
  899.0 65.2 reduce-scatter.38
  967.1 9.8 reduce-scatter.50
  979.8 11.0 reduce-scatter.52
  993.1 11.2 reduce-scatter.56
  1006.5 10.8 reduce-scatter.44
  1019.7 10.9 reduce-scatter.40
where the time goes:
time: 1040 us
  waiting for transfers between devices  744 us (72%)
  matrix products  130 us (12%)
  blocking collectives  78.6 us (8%)
  local copies, waits for them, and re-layouts  44.4 us (4%)
  other arithmetic  19.1 us (2%)
  between operations  16.1 us (2%)
    dot_general x35, matrix products, product(): return jnp.einsum(formula, left, right, preferred_element_type=jnp.float32)  130 us
    reduce_scatter x1, waiting for transfers between devices, local(): lax.psum_scatter(grad_up.astype(jnp.bfloat16), 'items', scatter_dimension...  64.9 us
    reduce_scatter x1, waiting for transfers between devices, local(): lax.psum_scatter(grad_gate.astype(jnp.bfloat16), 'items', scatter_dimensi...  64.3 us
    reduce_scatter x1, waiting for transfers between devices, local(): lax.psum_scatter(grad_down.astype(jnp.bfloat16), 'items', scatter_dimensi...  61.5 us
    reduce_scatter x1, waiting for transfers between devices, local(): lax.psum_scatter(grad_wq.astype(jnp.bfloat16), 'items', scatter_dimension...  58.9 us
    reduce_scatter x1, waiting for transfers between devices, local(): lax.psum_scatter(grad_wv.astype(jnp.bfloat16), 'items', scatter_dimension...  58.8 us
    reduce_scatter x1, waiting for transfers between devices, local(): lax.psum_scatter(grad_out.astype(jnp.bfloat16), 'items', scatter_dimensio...  53 us
    reduce_scatter x1, waiting for transfers between devices, local(): lax.psum_scatter(grad_wk.astype(jnp.bfloat16), 'items', scatter_dimension...  48.4 us
  transfers between devices with their start and end apart: 25, of which 22 were waited for; matrix products, arithmetic and copies ran while one was open for 12% of the time, Pallas kernels for 0%

commit v1 on v0

--- a/solution.py
+++ b/solution.py
@@ -1,6 +1,10 @@
+import functools
+
 import jax
 import jax.numpy as jnp
 from jax import lax
+from jax.experimental import pallas as pl
+from jax.experimental.pallas import tpu as pltpu
 from jax.sharding import PartitionSpec as P
 
 HEAD = 64
@@ -24,7 +28,7 @@
     return jnp.where(allowed[:, None, None, :], scores, -1000000000.0)
 
 
-def local(
+def general(
     patches,
     grid,
     norm_attn,
@@ -246,6 +250,300 @@
     )
 
 
+def swap_items(values, items, bit):
+    return lax.ppermute(values, "items", [(place, place ^ bit) for place in range(items)])
+
+
+def swap_blocks(values):
+    return lax.ppermute(values, "blk", [(0, 1), (1, 0)])
+
+
+def join(own, other, axis, later):
+    width = own.shape[axis]
+    shape = list(own.shape)
+    shape[axis] = 2 * width
+    whole = jnp.zeros(shape, own.dtype)
+    whole = lax.dynamic_update_slice_in_dim(whole, own, later * width, axis)
+    return lax.dynamic_update_slice_in_dim(whole, other, (1 - later) * width, axis)
+
+
+class Place:
+    def __init__(self, items):
+        self.items = items
+        self.levels = items.bit_length() - 1
+        self.index = lax.axis_index("items")
+        self.block = lax.axis_index("blk")
+
+    def bit(self, level):
+        return (self.index >> (self.levels - 1 - level)) & 1
+
+    def gather(self, shard, order):
+        rows, columns = shard.shape
+        whole = shard.reshape((1,) * self.levels + (rows, columns))
+        for step in order:
+            if step == "blk":
+                whole = join(whole, swap_blocks(whole), self.levels + 1, self.block)
+            else:
+                other = swap_items(whole, self.items, 1 << (self.levels - 1 - step))
+                whole = join(whole, other, step, self.bit(step))
+        return whole.reshape(-1, whole.shape[-1])
+
+    def scatter(self, whole, rows, order):
+        part = whole.reshape((2,) * self.levels + (rows, whole.shape[-1]))
+        for step in order:
+            if step == "blk":
+                axis, mine = self.levels + 1, self.block
+            else:
+                axis, mine = step, self.bit(step)
+            width = part.shape[axis] // 2
+            kept = lax.dynamic_slice_in_dim(part, mine * width, width, axis)
+            sent = lax.dynamic_slice_in_dim(part, (1 - mine) * width, width, axis)
+            if step == "blk":
+                other = swap_blocks(sent)
+            else:
+                other = swap_items(sent, self.items, 1 << (self.levels - 1 - step))
+            part = (kept.astype(jnp.float32) + other.astype(jnp.float32)).astype(jnp.bfloat16)
+        return part.reshape(rows, -1).astype(jnp.float32)
+
+    def total(self, values):
+        for level in range(self.levels):
+            values = values + swap_items(values, self.items, 1 << level)
+        return values + swap_blocks(values)
+
+
+def own_lanes(values, head):
+    lanes = lax.broadcasted_iota(jnp.int32, values.shape, 1)
+    return jnp.where(lanes // HEAD == head, values, jnp.zeros_like(values))
+
+
+def dot_nt(left, right):
+    return lax.dot_general(left, right, (((1,), (1,)), ((), ())), preferred_element_type=jnp.float32)
+
+
+def dot_tn(left, right):
+    return lax.dot_general(left, right, (((0,), (0,)), ((), ())), preferred_element_type=jnp.float32)
+
+
+def dot_nn(left, right):
+    return jnp.dot(left, right, preferred_element_type=jnp.float32)
+
+
+def attend_kernel(count_ref, q_ref, k_ref, v_ref, out_ref):
+    keys, values = k_ref[...], v_ref[...]
+    places = lax.broadcasted_iota(jnp.int32, (1, keys.shape[0]), 1)
+    bias = jnp.where(places < count_ref[0], 0.0, -1000000000.0)
+    total = None
+    for head in range(out_ref.shape[1] // HEAD):
+        scores = dot_nt(own_lanes(q_ref[...], head), keys) + bias
+        shifted = jnp.exp(scores - jnp.max(scores, -1, keepdims=True))
+        inverse = 1.0 / jnp.sum(shifted, -1, keepdims=True)
+        term = dot_nn((shifted * inverse).astype(jnp.bfloat16), values)
+        total = term if total is None else jnp.where(
+            lax.broadcasted_iota(jnp.int32, term.shape, 1) // HEAD == head, term, total
+        )
+    out_ref[...] = total.astype(jnp.bfloat16)
+
+
+def attend(count, qkv, rows=256):
+    length, width = qkv.shape[0], qkv.shape[1] // 3
+    groups = width // 128
+    return pl.pallas_call(
+        attend_kernel,
+        grid=(groups, length // rows),
+        in_specs=[
+            pl.BlockSpec(memory_space=pltpu.SMEM),
+            pl.BlockSpec((rows, 128), lambda g, r: (r, g)),
+            pl.BlockSpec((length, 128), lambda g, r: (0, groups + g)),
+            pl.BlockSpec((length, 128), lambda g, r: (0, 2 * groups + g)),
+        ],
+        out_specs=pl.BlockSpec((rows, 128), lambda g, r: (r, g)),
+        out_shape=jax.ShapeDtypeStruct((length, width), jnp.bfloat16),
+        compiler_params=pltpu.CompilerParams(vmem_limit_bytes=40 << 20),
+        name="attend",
+    )(count, qkv, qkv, qkv)
+
+
+def attend_back_kernel(count_ref, q_ref, k_ref, v_ref, grad_ref, dq_ref, dk_ref, dv_ref, dk_sum, dv_sum):
+    keys, values = k_ref[...], v_ref[...]
+    places = lax.broadcasted_iota(jnp.int32, (1, keys.shape[0]), 1)
+    bias = jnp.where(places < count_ref[0], 0.0, -1000000000.0)
+    grad_q = grad_k = grad_v = 0.0
+    for head in range(dq_ref.shape[1] // HEAD):
+        q_head = own_lanes(q_ref[...], head)
+        grad_head = own_lanes(grad_ref[...], head)
+        scores = dot_nt(q_head, keys) + bias
+        shifted = jnp.exp(scores - jnp.max(scores, -1, keepdims=True))
+        chances = shifted * (1.0 / jnp.sum(shifted, -1, keepdims=True))
+        grad_chances = dot_nt(grad_head, values)
+        weighed = chances * grad_chances
+        grad_scores = (weighed - chances * jnp.sum(weighed, -1, keepdims=True)).astype(jnp.bfloat16)
+        grad_q = grad_q + dot_nn(grad_scores, own_lanes(keys, head))
+        grad_k = grad_k + dot_tn(grad_scores, q_head)
+        grad_v = grad_v + dot_tn(chances.astype(jnp.bfloat16), grad_head)
+    dq_ref[...] = grad_q.astype(jnp.bfloat16)
+
+    @pl.when(pl.program_id(1) == 0)
+    def _():
+        dk_sum[...] = grad_k
+        dv_sum[...] = grad_v
+
+    @pl.when(pl.program_id(1) > 0)
+    def _():
+        dk_sum[...] += grad_k
+        dv_sum[...] += grad_v
+
+    @pl.when(pl.program_id(1) == pl.num_programs(1) - 1)
+    def _():
+        dk_ref[...] = dk_sum[...].astype(jnp.bfloat16)
+        dv_ref[...] = dv_sum[...].astype(jnp.bfloat16)
+
+
+def attend_back(count, qkv, grad, rows=256):
+    length, width = grad.shape
+    groups = width // 128
+    shape = jax.ShapeDtypeStruct((length, width), jnp.bfloat16)
+    return pl.pallas_call(
+        attend_back_kernel,
+        grid=(groups, length // rows),
+        in_specs=[
+            pl.BlockSpec(memory_space=pltpu.SMEM),
+            pl.BlockSpec((rows, 128), lambda g, r: (r, g)),
+            pl.BlockSpec((length, 128), lambda g, r: (0, groups + g)),
+            pl.BlockSpec((length, 128), lambda g, r: (0, 2 * groups + g)),
+            pl.BlockSpec((rows, 128), lambda g, r: (r, g)),
+        ],
+        out_specs=[
+            pl.BlockSpec((rows, 128), lambda g, r: (r, g)),
+            pl.BlockSpec((length, 128), lambda g, r: (0, g)),
+            pl.BlockSpec((length, 128), lambda g, r: (0, g)),
+        ],
+        out_shape=[shape, shape, shape],
+        scratch_shapes=[pltpu.VMEM((length, 128), jnp.float32), pltpu.VMEM((length, 128), jnp.float32)],
+        compiler_params=pltpu.CompilerParams(vmem_limit_bytes=40 << 20),
+        name="attend_back",
+    )(count, qkv, qkv, qkv, grad)
+
+
+def by_heads(
+    items,
+    patches,
+    grid,
+    norm_attn,
+    w_query,
+    w_key,
+    w_value,
+    w_out,
+    norm_mlp,
+    w_gate,
+    w_up,
+    w_down,
+    cotangent,
+):
+    place = Place(items)
+    levels, block = place.levels, place.block
+    far = list(range(levels - 2))
+    row_count, model_width = patches.shape[1:]
+    length = 2 * row_count
+    half = model_width // 2
+    count = (grid[:, 0] * grid[:, 1]).astype(jnp.int32)
+    own_rows, own_cot = patches[0], cotangent[0]
+    shard_rows, down_rows = w_query.shape[0], w_down.shape[0]
+
+    all_rows = join(own_rows, swap_blocks(own_rows), 0, block)
+    attn_weights = place.gather(
+        jnp.concatenate([w_query, w_key, w_value, w_out], 1), far + [levels - 2, levels - 1]
+    )
+    w_qkv, out_half = attn_weights[:, : 3 * half], attn_weights[:, 3 * half :]
+    full_gate = place.gather(w_gate, far + ["blk", levels - 2, levels - 1])
+    full_up = place.gather(w_up, far + [levels - 2, "blk", levels - 1])
+    full_down = place.gather(w_down, ["blk"] + far + [levels - 2, levels - 1])
+    full_out = join(out_half, swap_blocks(out_half), 1, block)
+
+    all_normed = rms_norm(all_rows.astype(jnp.float32), norm_attn).astype(jnp.bfloat16)
+    qkv = dot_nn(all_normed, w_qkv).astype(jnp.bfloat16)
+    attended_heads = attend(count, qkv)
+
+    def exchange_rows(values):
+        kept = lax.dynamic_slice_in_dim(values, block * row_count, row_count, 0)
+        sent = lax.dynamic_slice_in_dim(values, (1 - block) * row_count, row_count, 0)
+        return join(kept, swap_blocks(sent), 1, block)
+
+    def exchange_heads(values):
+        kept = lax.dynamic_slice_in_dim(values, block * half, half, 1)
+        sent = lax.dynamic_slice_in_dim(values, (1 - block) * half, half, 1)
+        return join(kept, swap_blocks(sent), 0, block)
+
+    attended = exchange_rows(attended_heads)
+    patch_rows = own_rows.astype(jnp.float32)
+    middle = patch_rows + dot_nn(attended, full_out)
+    normed_mlp = rms_norm(middle, norm_mlp).astype(jnp.bfloat16)
+    gate_in = dot_nn(normed_mlp, full_gate)
+    upward = dot_nn(normed_mlp, full_up)
+    activated = jax.nn.gelu(gate_in, approximate=True)
+    hidden = (activated * upward).astype(jnp.bfloat16)
+    output = (middle + dot_nn(hidden, full_down)).astype(jnp.bfloat16)
+    grad_down = dot_tn(hidden, own_cot).astype(jnp.bfloat16)
+    grad_hidden = dot_nt(own_cot, full_down)
+    unused_gelu, gelu_back = jax.vjp(lambda inner: jax.nn.gelu(inner, approximate=True), gate_in)
+    grad_gate_in = gelu_back(grad_hidden * upward)[0].astype(jnp.bfloat16)
+    grad_upward = (grad_hidden * activated).astype(jnp.bfloat16)
+    grad_gate = dot_tn(normed_mlp, grad_gate_in).astype(jnp.bfloat16)
+    grad_up = dot_tn(normed_mlp, grad_upward).astype(jnp.bfloat16)
+    grad_normed_mlp = dot_nt(grad_gate_in, full_gate) + dot_nt(grad_upward, full_up)
+    unused_norm, second_back = jax.vjp(rms_norm, middle, norm_mlp)
+    grad_middle_part, gain_mlp = second_back(grad_normed_mlp)
+    grad_middle = own_cot.astype(jnp.float32) + grad_middle_part
+    branch_grad = grad_middle.astype(jnp.bfloat16)
+    grad_attended = dot_nt(branch_grad, full_out).astype(jnp.bfloat16)
+    grad_out = dot_tn(attended, branch_grad).astype(jnp.bfloat16)
+    grad_heads = exchange_heads(grad_attended)
+    grad_qkv = jnp.concatenate(attend_back(count, qkv, grad_heads), 1)
+    grad_w_qkv = dot_tn(all_normed, grad_qkv).astype(jnp.bfloat16)
+    grad_all_normed = dot_nt(grad_qkv, w_qkv)
+    kept = lax.dynamic_slice_in_dim(grad_all_normed, block * row_count, row_count, 0)
+    sent = lax.dynamic_slice_in_dim(grad_all_normed, (1 - block) * row_count, row_count, 0)
+    grad_normed = kept + swap_blocks(sent.astype(jnp.bfloat16)).astype(jnp.float32)
+    unused_first, first_back = jax.vjp(rms_norm, patch_rows, norm_attn)
+    grad_rows_part, gain_attn = first_back(grad_normed)
+    grad_patches = (grad_middle + grad_rows_part).astype(jnp.bfloat16)
+
+    near = far[::-1]
+    shard_down = place.scatter(grad_down, down_rows, [levels - 1, levels - 2] + near + ["blk"])
+    shard_gate = place.scatter(grad_gate, shard_rows, [levels - 1, levels - 2, "blk"] + near)
+    shard_up = place.scatter(grad_up, shard_rows, [levels - 1, "blk", levels - 2] + near)
+    shard_out = place.scatter(grad_out, shard_rows, [levels - 1, "blk", levels - 2] + near)
+    shard_qkv = place.scatter(grad_w_qkv, shard_rows, [levels - 1, levels - 2] + near)
+    gains = lax.psum((gain_attn, gain_mlp), ("items", "blk"))
+    return (
+        output[None],
+        grad_patches[None],
+        gains[0],
+        shard_qkv[:, :half],
+        shard_qkv[:, half : 2 * half],
+        shard_qkv[:, 2 * half :],
+        shard_out,
+        gains[1],
+        shard_gate,
+        shard_up,
+        shard_down,
+    )
+
+
+def local(items, blocks, patches, *rest):
+    items_here, row_count, model_width = patches.shape
+    fits = (
+        blocks == 2
+        and items_here == 1
+        and items >= 8
+        and items & (items - 1) == 0
+        and row_count % 128 == 0
+        and model_width % 256 == 0
+    )
+    if fits:
+        return by_heads(items, patches, *rest)
+    return general(patches, *rest)
+
+
 def solution(mesh):
     placed = (
         P("items", "blk", None),
@@ -262,7 +560,7 @@
         P("items", "blk", None),
     )
     return jax.shard_map(
-        local,
+        functools.partial(local, mesh.shape["items"], mesh.shape["blk"]),
         mesh=mesh,
         in_specs=placed,
         out_specs=(

time: 1040 us -> 357 us (0.34)
  waiting for transfers between devices: 744 us -> 137 us
  matrix products: 130 us -> 38.4 us
  Pallas kernels: 0 us -> 48.4 us
  starting transfers between devices: 1.42 us -> 49.7 us
  blocking collectives: 78.6 us -> 39.4 us
  local copies, waits for them, and re-layouts: 44.4 us -> 15.7 us
  between operations: 16.1 us -> 3.7 us
    reduce_scatter x11 -> x0, waiting for transfers between devices: 469 us -> none  [the longest x1 64.9 us: local(): lax.psum_scatter(grad_up.astype(jnp.bfloat16), 'items', scatter_dimension...]
    all_gather x9 -> x0, waiting for transfers between devices: 256 us -> none  [the longest x1 42.8 us: local(): lax.all_gather(columns[5], 'items', axis=0, tiled=True)]
    ppermute x0 -> x48, waiting for transfers between devices: none -> 137 us  [the longest x36 97.7 us: swap_items(): lax.ppermute(values, 'items', [(place, place ^ bit) for place in range(it...]
    dot_general x35 -> x15, matrix products: 130 us -> 38.4 us  [the longest x5 18.3 us: dot_nn(): return jnp.dot(left, right, preferred_element_type=jnp.float32)]
    ppermute x0 -> x48, starting transfers between devices: none -> 49.7 us  [the longest x36 36.8 us: swap_items(): lax.ppermute(values, 'items', [(place, place ^ bit) for place in range(it...]
    pallas_call x0 -> x2, Pallas kernels: none -> 48.4 us  [the longest x1 30.7 us: attend_back(): pl.pallas_call(attend_back_kernel, grid=(groups, length // rows), in_spec...]
    all_gather x7 -> x0, blocking collectives: 38.8 us -> none  [the longest x1 7.22 us: local(): lax.all_gather(w_key, 'blk', axis=1, tiled=True)]
    unnamed x80 -> x46, local copies, waits for them, and re-layouts: 25.7 us -> 1.71 us
  transfers between devices with their start and end apart: 25 -> 48, of which waited for: 22 -> 29; matrix products, arithmetic and copies ran while one was open for 12% -> 13% of each run, Pallas kernels for 0% -> 14%
where the time goes in v1:
time: 357 us; the launch traced here: 351 us
  waiting for transfers between devices  137 us (38%)
  starting transfers between devices  49.7 us (14%)
  Pallas kernels  48.4 us (14%)
  blocking collectives  39.4 us (11%)
  matrix products  38.4 us (11%)
  other arithmetic  18.8 us (5%)
  local copies, waits for them, and re-layouts  15.7 us (4%)
  between operations  3.7 us (1%)
    ppermute x36, waiting for transfers between devices, swap_items(): lax.ppermute(values, 'items', [(place, place ^ bit) for place in range(it...  97.7 us
    psum x1, blocking collectives, by_heads(): gains = lax.psum((gain_attn, gain_mlp), ('items', 'blk'))  39.4 us
    ppermute x12, waiting for transfers between devices, swap_blocks(): return lax.ppermute(values, 'blk', [(0, 1), (1, 0)])  39.3 us
    ppermute x36, starting transfers between devices, swap_items(): lax.ppermute(values, 'items', [(place, place ^ bit) for place in range(it...  36.8 us
    pallas_call x1, Pallas kernels, attend_back(): pl.pallas_call(attend_back_kernel, grid=(groups, length // rows), in_spec...  30.7 us
    dot_general x5, matrix products, dot_nn(): return jnp.dot(left, right, preferred_element_type=jnp.float32)  18.3 us
    pallas_call x1, Pallas kernels, attend(): pl.pallas_call(attend_kernel, grid=(groups, length // rows), in_specs=[pl...  17.7 us
    ppermute x12, starting transfers between devices, swap_blocks(): return lax.ppermute(values, 'blk', [(0, 1), (1, 0)])  12.9 us
  transfers between devices with their start and end apart: 48, of which 29 were waited for; matrix products, arithmetic and copies ran while one was open for 13% of the time, Pallas kernels for 14%

profile of v1, /device:TPU:0, one launch (start us, length us, event | category | flops | bytes accessed | tf_op | source)
XLA Modules:
  0.0 351.2 jit_solution(18112761933037707681)
XLA Ops:
  0.7 4.1 %collective-permute-start.12 = (bf16[1,1,1,1,48,1024]{5,4,3,2,1,0:T(8,128)(2,1)}, bf16[1,1,1,1,48,1024]{5,4,3,2,1,0:T(8,128)(2,1)S(1)}, u32[]{:S(2)}, u32[]{:S(2)}) collective-permute-start(bf16[1,1,1,1,48,1024]{5,4,3,2,1,0:T(8,128)(2,1)} %bitcast.111), channel_id=1, source_target_pairs={{0,16},{2,18},{4,20},{6,22},{8,24},{10,26},{12,28},{14,30},{16,0},... | collective-permute-start | bytes 294920 | tf_op jit(solution)/shard_map/ppermute | solution.py:254
  5.7 1.8 collective-permute-start
  7.8 2.8 collective-permute-start.7
  10.7 1.4 fusion.14
  16.0 1.6 collective-permute-start.13
  17.6 9.5 %collective-permute-done.17 = bf16[1,1,1,1,128,384]{5,4,3,2,1,0:T(8,128)(2,1)S(1)} collective-permute-done((bf16[1,1,1,1,128,384]{5,4,3,2,1,0:T(8,128)(2,1)}, bf16[1,1,1,1,128,384]{5,4,3,2,1,0:T(8,128)(2,1)S(1)}, u32[]{:S(2)}, u32[]{:S(2)}) %collective-permute-start.17) | collective-permute-done | bytes 98336 | tf_op jit(solution)/shard_map/ppermute | solution.py:258
  27.1 2.6 collective-permute-start.18
  29.8 1.6 collective-permute-start.8
  32.3 1.6 collective-permute-start.14
  33.9 3.9 %collective-permute-done.18 = bf16[1,1,1,1,128,768]{5,4,3,2,1,0:T(8,128)(2,1)S(1)} collective-permute-done((bf16[1,1,1,1,128,768]{5,4,3,2,1,0:T(8,128)(2,1)S(1)}, bf16[1,1,1,1,128,768]{5,4,3,2,1,0:T(8,128)(2,1)S(1)}, u32[]{:S(2)}, u32[]{:S(2)}) %collective-permute-start.18) | collective-permute-done | bytes 196640 | tf_op jit(solution)/shard_map/ppermute | solution.py:254
  38.3 2.0 collective-permute-done.8
  41.9 4.7 %collective-permute-done.2 = bf16[2,1,1,1,48,1536]{5,4,3,2,1,0:T(8,128)(2,1)S(1)} collective-permute-done((bf16[2,1,1,1,48,1536]{5,4,3,2,1,0:T(8,128)(2,1)S(1)}, bf16[2,1,1,1,48,1536]{5,4,3,2,1,0:T(8,128)(2,1)S(1)}, u32[]{:S(2)}, u32[]{:S(2)}) %collective-permute-start.2) | collective-permute-done | bytes 294944 | tf_op jit(solution)/shard_map/ppermute | solution.py:254
  46.6 1.3 collective-permute-start.3
  48.2 1.6 collective-permute-start.15
  49.7 3.2 collective-permute-done.19
  56.3 5.6 %collective-permute-done.3 = bf16[2,2,1,1,48,1536]{5,4,3,2,1,0:T(8,128)(2,1)S(1)} collective-permute-done((bf16[2,2,1,1,48,1536]{5,4,3,2,1,0:T(8,128)(2,1)S(1)}, bf16[2,2,1,1,48,1536]{5,4,3,2,1,0:T(8,128)(2,1)S(1)}, u32[]{:S(2)}, u32[]{:S(2)}) %collective-permute-start.3) | collective-permute-done | bytes 589856 | tf_op jit(solution)/shard_map/ppermute | solution.py:254
  62.4 3.0 collective-permute-done.15
  65.6 13.2 %collective-permute-done.20 = bf16[2,2,1,1,128,768]{5,4,3,2,1,0:T(8,128)(2,1)S(1)} collective-permute-done((bf16[2,2,1,1,128,768]{5,4,3,2,1,0:T(8,128)(2,1)S(1)}, bf16[2,2,1,1,128,768]{5,4,3,2,1,0:T(8,128)(2,1)S(1)}, u32[]{:S(2)}, u32[]{:S(2)}) %collective-permute-start.20) | collective-permute-done | bytes 786464 | tf_op jit(solution)/shard_map/ppermute | solution.py:254
  78.9 12.6 %collective-permute-done.10 = bf16[2,2,1,1,48,2048]{5,4,3,2,1,0:T(8,128)(2,1)S(1)} collective-permute-done((bf16[2,2,1,1,48,2048]{5,4,3,2,1,0:T(8,128)(2,1)S(1)}, bf16[2,2,1,1,48,2048]{5,4,3,2,1,0:T(8,128)(2,1)S(1)}, u32[]{:S(2)}, u32[]{:S(2)}) %collective-permute-start.10) | collective-permute-done | bytes 786464 | tf_op jit(solution)/shard_map/ppermute | solution.py:254
  93.8 2.3 convolution_convert_fusion.q_ref.k_ref.v_ref
  96.2 17.7 %attend.1 = bf16[1024,384]{1,0:T(8,128)(2,1)S(1)} custom-call(s32[1]{0:T(128)} %bitcast.1.count_ref, bf16[1024,1152]{1,0:T(8,128)(2,1)S(1)} %convolution_convert_fusion.q_ref.k_ref.v_ref, bf16[1024,1152]{1,0:T(8,128)(2,1)S(1)} %convolution_convert_fusion.q_ref.k_ref.v_ref, bf16[1024,1152]{1,0:T(8,128)(2,1)S(1)} %convolution_convert_fusion.q_ref.k_ref.v_ref), custom_call_target="tpu_custom_call" | custom-call | tf_op jit(solution)/shard_map/attend/pallas_call | solution.py:350
  116.0 5.9 %collective-permute-done.5 = bf16[512,384]{1,0:T(8,128)(2,1)S(1)} collective-permute-done((bf16[512,384]{1,0:T(8,128)(2,1)S(1)}, bf16[512,384]{1,0:T(8,128)(2,1)S(1)}, u32[]{:S(2)}, u32[]{:S(2)}) %collective-permute-start.5) | collective-permute-done | bytes 393248 | tf_op jit(solution)/shard_map/ppermute | solution.py:258
  123.7 3.8 %fusion.45 = f32[512,2048]{1,0:T(8,128)} fusion(bf16[512,768]{1,0:T(8,128)(2,1)S(1)} %multiply_convert_fusion.1, bf16[768,2048]{1,0:T(8,128)(2,1)S(1)} %bitcast.103), kind=kOutput, calls=%fused_computation.178 | convolution fusion | flops 1610612736 | bytes 8126464 | tf_op jit(solution)/shard_map/dot_general | solution.py:328
  127.5 3.8 %fusion.24 = f32[2048,512]{0,1:T(8,128)} fusion(bf16[2048,768]{1,0:T(8,128)(2,1)S(1)} %bitcast.105, bf16[1,512,768]{2,1,0:T(8,128)(2,1)S(1)} %copy-done.10), kind=kOutput, calls=%fused_computation.63 | convolution fusion | flops 1610612736 | bytes 8126464 | tf_op jit(solution)/shard_map/dot_general | solution.py:320
  131.5 8.5 %fusion.6 = (bf16[512,2048]{1,0:T(8,128)(2,1)S(1)}, bf16[512,2048]{1,0:T(8,128)(2,1)S(1)}, bf16[512,2048]{1,0:T(8,128)(2,1)}) fusion(f32[512,2048]{1,0:T(8,128)} %fusion.45, f32[2048,512]{0,1:T(8,128)} %fusion.24, bf16[512,768]{1,0:T(8,128)(2,1)S(1)} %multiply_convert_fusion.1, bf16[768,2048]{1,0:T(8,128)(2,1)S(1)} %bitcast.107), kind=kOutput, calls=%fused_computation.8 | convolution fusion | flops 1637875712 | bytes 18612224 | tf_op jit(solution)/shard_map/dot_general | solution.py:328
  140.0 1.9 convolution_convert_fusion.2
  141.9 1.9 fusion.46
  143.8 1.9 convolution_convert_fusion.3
  145.6 2.7 multiply_reduce_fusion
  151.2 1.9 convolution_convert_fusion.1
  153.1 2.7 fusion.21
  158.0 1.3 constant_dynamic-slice_fusion.9
  160.2 1.3 constant_dynamic-slice_fusion.14
  161.8 7.0 %collective-permute-done.22 = bf16[512,384]{1,0:T(8,128)(2,1)S(1)} collective-permute-done((bf16[512,384]{1,0:T(8,128)(2,1)S(1)}, bf16[512,384]{1,0:T(8,128)(2,1)S(1)}, u32[]{:S(2)}, u32[]{:S(2)}) %collective-permute-start.22) | collective-permute-done | bytes 393248 | tf_op jit(solution)/shard_map/ppermute | solution.py:258
  168.9 30.7 %attend_back.1 = (bf16[1024,384]{1,0:T(8,128)(2,1)S(1)}, bf16[1024,384]{1,0:T(8,128)(2,1)S(1)}, bf16[1024,384]{1,0:T(8,128)(2,1)S(1)}) custom-call(s32[1]{0:T(128)} %bitcast.1.count_ref, bf16[1024,1152]{1,0:T(8,128)(2,1)S(1)} %convolution_convert_fusion.q_ref.k_ref.v_ref, bf16[1024,1152]{1,0:T(8,128)(2,1)S(1)} %convolution_convert_fusion.q_ref.k_ref.v_ref, ...), custom_call_target="tpu_custom_call" | custom-call | tf_op jit(solution)/shard_map/attend_back/pallas_call | solution.py:405
  201.0 2.2 fusion.18
  203.3 5.7 %collective-permute-done.29 = bf16[2,2,2,1,48,384]{5,4,3,2,1,0:T(8,128)(2,1)S(1)} collective-permute-done((bf16[2,2,2,1,48,384]{5,4,3,2,1,0:T(8,128)(2,1)S(1)}, bf16[2,2,2,1,48,384]{5,4,3,2,1,0:T(8,128)(2,1)S(1)}, u32[]{:S(2)}, u32[]{:S(2)}) %collective-permute-start.29) | collective-permute-done | bytes 294944 | tf_op jit(solution)/shard_map/ppermute | solution.py:258
  209.1 1.6 collective-permute-start.30
  210.7 2.4 convolution_convert_fusion.4
  215.9 2.9 collective-permute-done.31
  220.7 3.0 collective-permute-done.32
  224.4 7.8 %collective-permute-done.23 = bf16[512,768]{1,0:T(8,128)(2,1)S(1)} collective-permute-done((bf16[512,768]{1,0:T(8,128)(2,1)S(1)}, bf16[512,768]{1,0:T(8,128)(2,1)S(1)}, u32[]{:S(2)}, u32[]{:S(2)}) %collective-permute-start.23) | collective-permute-done | bytes 786464 | tf_op jit(solution)/shard_map/ppermute | solution.py:258
  233.0 39.4 %all-reduce = (f32[768]{0:T(1024)}, f32[768]{0:T(1024)}) all-reduce(f32[768]{0:T(1024)S(1)} %get-tuple-element.17, f32[768]{0:T(1024)S(1)} %copy-done.19), channel_id=1, replica_groups=mesh['items'=16,'blk'=2] {'items','blk'}, use_global_device_ids=true, to_apply=%region_6.0 | all-reduce | flops 1536 | bytes 12288 | tf_op jit(solution)/shard_map/psum | solution.py:516
  272.4 3.0 fusion.22
  275.4 1.5 add_convert_fusion.3
  277.0 2.6 collective-permute-start.25
  279.6 1.9 add_convert_fusion
  282.2 1.9 add_convert_fusion.1
  284.1 1.6 collective-permute-start.39
  285.7 5.0 %collective-permute-done.25 = bf16[2,2,1,1,48,1152]{5,4,3,2,1,0:T(8,128)(2,1)S(1)} collective-permute-done((bf16[2,2,1,1,48,1152]{5,4,3,2,1,0:T(8,128)(2,1)S(1)}, bf16[2,2,1,1,48,1152]{5,4,3,2,1,0:T(8,128)(2,1)S(1)}, u32[]{:S(2)}, u32[]{:S(2)}) %collective-permute-start.25) | collective-permute-done | bytes 442400 | tf_op jit(solution)/shard_map/ppermute | solution.py:254
  291.7 1.9 add_convert_fusion.2
  293.6 4.0 %collective-permute-done.26 = bf16[2,1,1,1,48,1152]{5,4,3,2,1,0:T(8,128)(2,1)S(1)} collective-permute-done((bf16[2,1,1,1,48,1152]{5,4,3,2,1,0:T(8,128)(2,1)S(1)}, bf16[2,1,1,1,48,1152]{5,4,3,2,1,0:T(8,128)(2,1)S(1)}, u32[]{:S(2)}, u32[]{:S(2)}) %collective-permute-start.26) | collective-permute-done | bytes 221216 | tf_op jit(solution)/shard_map/ppermute | solution.py:254
  298.3 2.7 collective-permute-start.34
  301.0 3.6 %collective-permute-done.27 = bf16[1,1,1,1,48,1152]{5,4,3,2,1,0:T(8,128)(2,1)S(1)} collective-permute-done((bf16[1,1,1,1,48,1152]{5,4,3,2,1,0:T(8,128)(2,1)S(1)}, bf16[1,1,1,1,48,1152]{5,4,3,2,1,0:T(8,128)(2,1)S(1)}, u32[]{:S(2)}, u32[]{:S(2)}) %collective-permute-start.27) | collective-permute-done | bytes 110624 | tf_op jit(solution)/shard_map/ppermute | solution.py:254
  305.2 2.3 collective-permute-done.44
  309.0 2.1 collective-permute-start.40
  311.0 13.3 %collective-permute-done.34 = bf16[2,2,1,1,48,2048]{5,4,3,2,1,0:T(8,128)(2,1)S(1)} collective-permute-done((bf16[2,2,1,1,48,2048]{5,4,3,2,1,0:T(8,128)(2,1)S(1)}, bf16[2,2,1,1,48,2048]{5,4,3,2,1,0:T(8,128)(2,1)S(1)}, u32[]{:S(2)}, u32[]{:S(2)}) %collective-permute-start.34) | collective-permute-done | bytes 786464 | tf_op jit(solution)/shard_map/ppermute | solution.py:254
  324.7 1.8 collective-permute-start.35
  327.6 3.6 %collective-permute-done.40 = bf16[2,2,1,1,48,1024]{5,4,3,2,1,0:T(8,128)(2,1)S(1)} collective-permute-done((bf16[2,2,1,1,48,1024]{5,4,3,2,1,0:T(8,128)(2,1)S(1)}, bf16[2,2,1,1,48,1024]{5,4,3,2,1,0:T(8,128)(2,1)S(1)}, u32[]{:S(2)}, u32[]{:S(2)}) %collective-permute-start.40) | collective-permute-done | bytes 393248 | tf_op jit(solution)/shard_map/ppermute | solution.py:254
  333.7 1.8 collective-permute-done.46
  335.9 3.8 %collective-permute-done.41 = bf16[2,1,1,1,48,1024]{5,4,3,2,1,0:T(8,128)(2,1)S(1)} collective-permute-done((bf16[2,1,1,1,48,1024]{5,4,3,2,1,0:T(8,128)(2,1)S(1)}, bf16[2,1,1,1,48,1024]{5,4,3,2,1,0:T(8,128)(2,1)S(1)}, u32[]{:S(2)}, u32[]{:S(2)}) %collective-permute-start.41) | collective-permute-done | bytes 196640 | tf_op jit(solution)/shard_map/ppermute | solution.py:254
  340.3 3.5 collective-permute-done.36
  344.8 2.1 collective-permute-done.42
  347.6 2.4 collective-permute-done.37
  (229 shorter events, 42.8 us)
Async XLA Ops:
  0.6 12.4 %copy-start.14 = (bf16[48,384]{1,0:T(8,128)(2,1)S(1)}, bf16[48,384]{1,0:T(8,128)(2,1)}, u32[]{:S(2)}) copy-start(bf16[48,384]{1,0:T(8,128)(2,1)} %param.15) | copy-start | bytes 110596
  0.7 12.4 %copy-start.13 = (bf16[48,384]{1,0:T(8,128)(2,1)S(1)}, bf16[48,384]{1,0:T(8,128)(2,1)}, u32[]{:S(2)}) copy-start(bf16[48,384]{1,0:T(8,128)(2,1)} %param.16) | copy-start | bytes 110596
  0.7 12.4 %copy-start.12 = (bf16[48,384]{1,0:T(8,128)(2,1)S(1)}, bf16[48,384]{1,0:T(8,128)(2,1)}, u32[]{:S(2)}) copy-start(bf16[48,384]{1,0:T(8,128)(2,1)} %param.17) | copy-start | bytes 110596
  0.7 12.4 %copy-start.11 = (bf16[48,384]{1,0:T(8,128)(2,1)S(1)}, bf16[48,384]{1,0:T(8,128)(2,1)}, u32[]{:S(2)}) copy-start(bf16[48,384]{1,0:T(8,128)(2,1)} %param.18) | copy-start | bytes 110596
  0.7 12.5 %copy-start.16 = (bf16[48,1024]{1,0:T(8,128)(2,1)S(1)}, bf16[48,1024]{1,0:T(8,128)(2,1)}, u32[]{:S(2)}) copy-start(bf16[48,1024]{1,0:T(8,128)(2,1)} %param.20) | copy-start | bytes 294916
  0.7 15.3 %collective-permute-start.12 = (bf16[1,1,1,1,48,1024]{5,4,3,2,1,0:T(8,128)(2,1)}, bf16[1,1,1,1,48,1024]{5,4,3,2,1,0:T(8,128)(2,1)S(1)}, u32[]{:S(2)}, u32[]{:S(2)}) collective-permute-start(bf16[1,1,1,1,48,1024]{5,4,3,2,1,0:T(8,128)(2,1)} %bitcast.111), channel_id=1, source_target_pairs={{0,16},{2,18},{4,20},{6,22},{8,24},{10,26},{12,28},{14,30},{16,0},... | collective-permute-start | bytes 294920 | tf_op jit(solution)/shard_map/ppermute | solution.py:254
  5.6 26.0 %collective-permute-start.1 = (bf16[1,1,1,1,48,1536]{5,4,3,2,1,0:T(8,128)(2,1)S(1)}, bf16[1,1,1,1,48,1536]{5,4,3,2,1,0:T(8,128)(2,1)S(1)}, u32[]{:S(2)}, u32[]{:S(2)}) collective-permute-start(bf16[1,1,1,1,48,1536]{5,4,3,2,1,0:T(8,128)(2,1)S(1)} %maximum_bitcast_fusion), channel_id=1, source_target_pairs={{0,16},{2,18},{4,20},{6,22},{8,24},{10,26},{12,28},{14,30},{16,0},... | collective-permute-start | bytes 442376 | tf_op jit(solution)/shard_map/ppermute | solution.py:254
  5.7 50.1 %collective-permute-start = (bf16[512,768]{1,0:T(8,128)(2,1)}, bf16[512,768]{1,0:T(8,128)(2,1)S(1)}, u32[]{:S(2)}, u32[]{:S(2)}) collective-permute-start(bf16[512,768]{1,0:T(8,128)(2,1)} %bitcast.91), channel_id=1, source_target_pairs={{0,1},{1,0},{2,3},{3,2},{4,5},{5,4},{6,7},{7,6},{8,9},{9,8},{10,11... | collective-permute-start | bytes 2359304 | tf_op jit(solution)/shard_map/ppermute | solution.py:258
  7.5 19.6 %collective-permute-start.17 = (bf16[1,1,1,1,128,384]{5,4,3,2,1,0:T(8,128)(2,1)}, bf16[1,1,1,1,128,384]{5,4,3,2,1,0:T(8,128)(2,1)S(1)}, u32[]{:S(2)}, u32[]{:S(2)}) collective-permute-start(bf16[1,1,1,1,128,384]{5,4,3,2,1,0:T(8,128)(2,1)} %bitcast.112), channel_id=1, source_target_pairs={{0,1},{1,0},{2,3},{3,2},{4,5},{5,4},{6,7},{7,6},{8,9},{9,8},{10,11... | collective-permute-start | bytes 294920 | tf_op jit(solution)/shard_map/ppermute | solution.py:258
  7.8 22.0 %collective-permute-start.7 = (bf16[1,1,1,1,48,1024]{5,4,3,2,1,0:T(8,128)(2,1)}, bf16[1,1,1,1,48,1024]{5,4,3,2,1,0:T(8,128)(2,1)S(1)}, u32[]{:S(2)}, u32[]{:S(2)}) collective-permute-start(bf16[1,1,1,1,48,1024]{5,4,3,2,1,0:T(8,128)(2,1)} %bitcast.113), channel_id=1, source_target_pairs={{0,16},{2,18},{4,20},{6,22},{8,24},{10,26},{12,28},{14,30},{16,0},... | collective-permute-start | bytes 294920 | tf_op jit(solution)/shard_map/ppermute | solution.py:254
  10.7 2.7 copy-start
  16.0 16.2 %collective-permute-start.13 = (bf16[2,1,1,1,48,1024]{5,4,3,2,1,0:T(8,128)(2,1)S(1)}, bf16[2,1,1,1,48,1024]{5,4,3,2,1,0:T(8,128)(2,1)S(1)}, u32[]{:S(2)}, u32[]{:S(2)}) collective-permute-start(bf16[2,1,1,1,48,1024]{5,4,3,2,1,0:T(8,128)(2,1)S(1)} %constant_dynamic-update-slice_fusion.19), channel_id=1, source_target_pairs={{0,8},{2,10},{4,12},{6,14},{8,0},{10,2},{12,4},{14,6},{16,24},{18,... | collective-permute-start | bytes 589832 | tf_op jit(solution)/shard_map/ppermute | solution.py:254
  27.1 10.7 %collective-permute-start.18 = (bf16[1,1,1,1,128,768]{5,4,3,2,1,0:T(8,128)(2,1)S(1)}, bf16[1,1,1,1,128,768]{5,4,3,2,1,0:T(8,128)(2,1)S(1)}, u32[]{:S(2)}, u32[]{:S(2)}) collective-permute-start(bf16[1,1,1,1,128,768]{5,4,3,2,1,0:T(8,128)(2,1)S(1)} %constant_dynamic-update-slice_fusion.9), channel_id=1, source_target_pairs={{0,16},{2,18},{4,20},{6,22},{8,24},{10,26},{12,28},{14,30},{16,0},... | collective-permute-start | bytes 589832 | tf_op jit(solution)/shard_map/ppermute | solution.py:254
  29.8 10.4 %collective-permute-start.8 = (bf16[2,1,1,1,48,1024]{5,4,3,2,1,0:T(8,128)(2,1)S(1)}, bf16[2,1,1,1,48,1024]{5,4,3,2,1,0:T(8,128)(2,1)S(1)}, u32[]{:S(2)}, u32[]{:S(2)}) collective-permute-start(bf16[2,1,1,1,48,1024]{5,4,3,2,1,0:T(8,128)(2,1)S(1)} %constant_dynamic-update-slice_fusion.29), channel_id=1, source_target_pairs={{0,8},{2,10},{4,12},{6,14},{8,0},{10,2},{12,4},{14,6},{16,24},{18,... | collective-permute-start | bytes 589832 | tf_op jit(solution)/shard_map/ppermute | solution.py:254
  31.7 14.9 %collective-permute-start.2 = (bf16[2,1,1,1,48,1536]{5,4,3,2,1,0:T(8,128)(2,1)S(1)}, bf16[2,1,1,1,48,1536]{5,4,3,2,1,0:T(8,128)(2,1)S(1)}, u32[]{:S(2)}, u32[]{:S(2)}) collective-permute-start(bf16[2,1,1,1,48,1536]{5,4,3,2,1,0:T(8,128)(2,1)S(1)} %constant_dynamic-update-slice_fusion.40), channel_id=1, source_target_pairs={{0,8},{2,10},{4,12},{6,14},{8,0},{10,2},{12,4},{14,6},{16,24},{18,... | collective-permute-start | bytes 884744 | tf_op jit(solution)/shard_map/ppermute | solution.py:254
  32.3 15.8 %collective-permute-start.14 = (bf16[2,2,1,1,48,1024]{5,4,3,2,1,0:T(8,128)(2,1)S(1)}, bf16[2,2,1,1,48,1024]{5,4,3,2,1,0:T(8,128)(2,1)S(1)}, u32[]{:S(2)}, u32[]{:S(2)}) collective-permute-start(bf16[2,2,1,1,48,1024]{5,4,3,2,1,0:T(8,128)(2,1)S(1)} %constant_dynamic-update-slice_fusion.17), channel_id=1, source_target_pairs={{0,4},{2,6},{4,0},{6,2},{8,12},{10,14},{12,8},{14,10},{16,20},{18,... | collective-permute-start | bytes 1179656 | tf_op jit(solution)/shard_map/ppermute | solution.py:254
  37.8 15.1 %collective-permute-start.19 = (bf16[2,1,1,1,128,768]{5,4,3,2,1,0:T(8,128)(2,1)S(1)}, bf16[2,1,1,1,128,768]{5,4,3,2,1,0:T(8,128)(2,1)S(1)}, u32[]{:S(2)}, u32[]{:S(2)}) collective-permute-start(bf16[2,1,1,1,128,768]{5,4,3,2,1,0:T(8,128)(2,1)S(1)} %constant_dynamic-update-slice_fusion.7), channel_id=1, source_target_pairs={{0,8},{2,10},{4,12},{6,14},{8,0},{10,2},{12,4},{14,6},{16,24},{18,... | collective-permute-start | bytes 1179656 | tf_op jit(solution)/shard_map/ppermute | solution.py:254
  40.3 14.4 %collective-permute-start.9 = (bf16[2,2,1,1,48,1024]{5,4,3,2,1,0:T(8,128)(2,1)S(1)}, bf16[2,2,1,1,48,1024]{5,4,3,2,1,0:T(8,128)(2,1)S(1)}, u32[]{:S(2)}, u32[]{:S(2)}) collective-permute-start(bf16[2,2,1,1,48,1024]{5,4,3,2,1,0:T(8,128)(2,1)S(1)} %constant_dynamic-update-slice_fusion.27), channel_id=1, source_target_pairs={{0,1},{1,0},{2,3},{3,2},{4,5},{5,4},{6,7},{7,6},{8,9},{9,8},{10,11... | collective-permute-start | bytes 1179656 | tf_op jit(solution)/shard_map/ppermute | solution.py:258
  46.6 15.3 %collective-permute-start.3 = (bf16[2,2,1,1,48,1536]{5,4,3,2,1,0:T(8,128)(2,1)S(1)}, bf16[2,2,1,1,48,1536]{5,4,3,2,1,0:T(8,128)(2,1)S(1)}, u32[]{:S(2)}, u32[]{:S(2)}) collective-permute-start(bf16[2,2,1,1,48,1536]{5,4,3,2,1,0:T(8,128)(2,1)S(1)} %constant_dynamic-update-slice_fusion.38), channel_id=1, source_target_pairs={{0,4},{2,6},{4,0},{6,2},{8,12},{10,14},{12,8},{14,10},{16,20},{18,... | collective-permute-start | bytes 1769480 | tf_op jit(solution)/shard_map/ppermute | solution.py:254
  48.2 17.3 %collective-permute-start.15 = (bf16[2,2,2,1,48,1024]{5,4,3,2,1,0:T(8,128)(2,1)S(1)}, bf16[2,2,2,1,48,1024]{5,4,3,2,1,0:T(8,128)(2,1)S(1)}, u32[]{:S(2)}, u32[]{:S(2)}) collective-permute-start(bf16[2,2,2,1,48,1024]{5,4,3,2,1,0:T(8,128)(2,1)S(1)} %constant_dynamic-update-slice_fusion.15), channel_id=1, source_target_pairs={{0,1},{1,0},{2,3},{3,2},{4,5},{5,4},{6,7},{7,6},{8,9},{9,8},{10,11... | collective-permute-start | bytes 2359304 | tf_op jit(solution)/shard_map/ppermute | solution.py:258
  52.9 25.8 %collective-permute-start.20 = (bf16[2,2,1,1,128,768]{5,4,3,2,1,0:T(8,128)(2,1)S(1)}, bf16[2,2,1,1,128,768]{5,4,3,2,1,0:T(8,128)(2,1)S(1)}, u32[]{:S(2)}, u32[]{:S(2)}) collective-permute-start(bf16[2,2,1,1,128,768]{5,4,3,2,1,0:T(8,128)(2,1)S(1)} %constant_dynamic-update-slice_fusion.5), channel_id=1, source_target_pairs={{0,4},{2,6},{4,0},{6,2},{8,12},{10,14},{12,8},{14,10},{16,20},{18,... | collective-permute-start | bytes 2359304 | tf_op jit(solution)/shard_map/ppermute | solution.py:254
  54.8 36.7 %collective-permute-start.10 = (bf16[2,2,1,1,48,2048]{5,4,3,2,1,0:T(8,128)(2,1)S(1)}, bf16[2,2,1,1,48,2048]{5,4,3,2,1,0:T(8,128)(2,1)S(1)}, u32[]{:S(2)}, u32[]{:S(2)}) collective-permute-start(bf16[2,2,1,1,48,2048]{5,4,3,2,1,0:T(8,128)(2,1)S(1)} %constant_dynamic-update-slice_fusion.25), channel_id=1, source_target_pairs={{0,4},{2,6},{4,0},{6,2},{8,12},{10,14},{12,8},{14,10},{16,20},{18,... | collective-permute-start | bytes 2359304 | tf_op jit(solution)/shard_map/ppermute | solution.py:254
  62.0 30.2 %collective-permute-start.4 = (bf16[2,2,2,1,48,1536]{5,4,3,2,1,0:T(8,128)(2,1)S(1)}, bf16[2,2,2,1,48,1536]{5,4,3,2,1,0:T(8,128)(2,1)S(1)}, u32[]{:S(2)}, u32[]{:S(2)}) collective-permute-start(bf16[2,2,2,1,48,1536]{5,4,3,2,1,0:T(8,128)(2,1)S(1)} %constant_dynamic-update-slice_fusion.36), channel_id=1, source_target_pairs={{0,2},{2,0},{4,6},{6,4},{8,10},{10,8},{12,14},{14,12},{16,18},{18,... | collective-permute-start | bytes 3538952 | tf_op jit(solution)/shard_map/ppermute | solution.py:254
  65.5 57.9 %collective-permute-start.16 = (bf16[2,2,2,1,48,2048]{5,4,3,2,1,0:T(8,128)(2,1)S(1)}, bf16[2,2,2,1,48,2048]{5,4,3,2,1,0:T(8,128)(2,1)S(1)}, u32[]{:S(2)}, u32[]{:S(2)}) collective-permute-start(bf16[2,2,2,1,48,2048]{5,4,3,2,1,0:T(8,128)(2,1)S(1)} %constant_dynamic-update-slice_fusion.13), channel_id=1, source_target_pairs={{0,2},{2,0},{4,6},{6,4},{8,10},{10,8},{12,14},{14,12},{16,18},{18,... | collective-permute-start | bytes 4718600 | tf_op jit(solution)/shard_map/ppermute | solution.py:254
  78.8 44.4 %collective-permute-start.21 = (bf16[2,2,2,1,128,768]{5,4,3,2,1,0:T(8,128)(2,1)S(1)}, bf16[2,2,2,1,128,768]{5,4,3,2,1,0:T(8,128)(2,1)S(1)}, u32[]{:S(2)}, u32[]{:S(2)}) collective-permute-start(bf16[2,2,2,1,128,768]{5,4,3,2,1,0:T(8,128)(2,1)S(1)} %constant_dynamic-update-slice_fusion.3), channel_id=1, source_target_pairs={{0,2},{2,0},{4,6},{6,4},{8,10},{10,8},{12,14},{14,12},{16,18},{18,... | collective-permute-start | bytes 4718600 | tf_op jit(solution)/shard_map/ppermute | solution.py:254
  92.6 29.4 %collective-permute-start.6 = (bf16[768,384]{1,0:T(8,128)(2,1)S(1)}, bf16[768,384]{1,0:T(8,128)(2,1)S(1)}, u32[]{:S(2)}, u32[]{:S(2)}) collective-permute-start(bf16[768,384]{1,0:T(8,128)(2,1)S(1)} %get-tuple-element.26), channel_id=1, source_target_pairs={{0,1},{1,0},{2,3},{3,2},{4,5},{5,4},{6,7},{7,6},{8,9},{9,8},{10,11... | collective-permute-start | bytes 1769480 | tf_op jit(solution)/shard_map/ppermute | solution.py:258
  114.1 7.8 %collective-permute-start.5 = (bf16[512,384]{1,0:T(8,128)(2,1)S(1)}, bf16[512,384]{1,0:T(8,128)(2,1)S(1)}, u32[]{:S(2)}, u32[]{:S(2)}) collective-permute-start(bf16[512,384]{1,0:T(8,128)(2,1)S(1)} %get-tuple-element.30), channel_id=1, source_target_pairs={{0,1},{1,0},{2,3},{3,2},{4,5},{5,4},{6,7},{7,6},{8,9},{9,8},{10,11... | collective-permute-start | bytes 1179656 | tf_op jit(solution)/shard_map/ppermute | solution.py:258
  115.4 15.9 %collective-permute-start.11 = (bf16[2,2,2,1,48,2048]{5,4,3,2,1,0:T(8,128)(2,1)S(1)}, bf16[2,2,2,1,48,2048]{5,4,3,2,1,0:T(8,128)(2,1)S(1)}, u32[]{:S(2)}, u32[]{:S(2)}) collective-permute-start(bf16[2,2,2,1,48,2048]{5,4,3,2,1,0:T(8,128)(2,1)S(1)} %constant_dynamic-update-slice_fusion.23), channel_id=1, source_target_pairs={{0,2},{2,0},{4,6},{6,4},{8,10},{10,8},{12,14},{14,12},{16,18},{18,... | collective-permute-start | bytes 4718600 | tf_op jit(solution)/shard_map/ppermute | solution.py:254
  123.6 3.8 %copy-start.10 = (bf16[1,512,768]{2,1,0:T(8,128)(2,1)S(1)}, bf16[1,512,768]{2,1,0:T(8,128)(2,1)}, u32[]{:S(2)}) copy-start(bf16[1,512,768]{2,1,0:T(8,128)(2,1)} %param.23) | copy-start | bytes 2359300
  141.9 16.1 %copy-start.4 = (bf16[768,2048]{1,0:T(8,128)(2,1)}, bf16[768,2048]{1,0:T(8,128)(2,1)S(1)}, u32[]{:S(2)}) copy-start(bf16[768,2048]{1,0:T(8,128)(2,1)S(1)} %convolution_convert_fusion.2) | copy-start | bytes 9437188
  145.6 14.6 %copy-start.2 = (bf16[768,2048]{1,0:T(8,128)(2,1)}, bf16[768,2048]{1,0:T(8,128)(2,1)S(1)}, u32[]{:S(2)}) copy-start(bf16[768,2048]{1,0:T(8,128)(2,1)S(1)} %convolution_convert_fusion.3) | copy-start | bytes 9437188
  153.0 2.7 copy-start.6
  157.0 122.6 %collective-permute-start.43 = (bf16[2,2,2,1,128,768]{5,4,3,2,1,0:T(8,128)(2,1)}, bf16[2,2,2,1,128,768]{5,4,3,2,1,0:T(8,128)(2,1)}, u32[]{:S(2)}, u32[]{:S(2)}) collective-permute-start(bf16[2,2,2,1,128,768]{5,4,3,2,1,0:T(8,128)(2,1)} %constant_dynamic-slice_fusion.4), channel_id=1, source_target_pairs={{0,2},{2,0},{4,6},{6,4},{8,10},{10,8},{12,14},{14,12},{16,18},{18,... | collective-permute-start | bytes 4718600 | tf_op jit(solution)/shard_map/ppermute | solution.py:254
  157.2 11.6 %collective-permute-start.22 = (bf16[512,384]{1,0:T(8,128)(2,1)S(1)}, bf16[512,384]{1,0:T(8,128)(2,1)S(1)}, u32[]{:S(2)}, u32[]{:S(2)}) collective-permute-start(bf16[512,384]{1,0:T(8,128)(2,1)S(1)} %get-tuple-element.28), channel_id=1, source_target_pairs={{0,1},{1,0},{2,3},{3,2},{4,5},{5,4},{6,7},{7,6},{8,9},{9,8},{10,11... | collective-permute-start | bytes 1179656 | tf_op jit(solution)/shard_map/ppermute | solution.py:258
  159.4 122.8 %collective-permute-start.38 = (bf16[2,2,2,1,48,2048]{5,4,3,2,1,0:T(8,128)(2,1)}, bf16[2,2,2,1,48,2048]{5,4,3,2,1,0:T(8,128)(2,1)}, u32[]{:S(2)}, u32[]{:S(2)}) collective-permute-start(bf16[2,2,2,1,48,2048]{5,4,3,2,1,0:T(8,128)(2,1)} %constant_dynamic-slice_fusion.9), channel_id=1, source_target_pairs={{0,2},{2,0},{4,6},{6,4},{8,10},{10,8},{12,14},{14,12},{16,18},{18,... | collective-permute-start | bytes 4718600 | tf_op jit(solution)/shard_map/ppermute | solution.py:254
  159.9 40.1 %collective-permute-start.28 = (bf16[2,2,2,1,48,768]{5,4,3,2,1,0:T(8,128)(2,1)S(1)}, bf16[2,2,2,1,48,768]{5,4,3,2,1,0:T(8,128)(2,1)S(1)}, u32[]{:S(2)}, u32[]{:S(2)}) collective-permute-start(bf16[2,2,2,1,48,768]{5,4,3,2,1,0:T(8,128)(2,1)S(1)} %constant_dynamic-slice_fusion.19), channel_id=1, source_target_pairs={{0,2},{2,0},{4,6},{6,4},{8,10},{10,8},{12,14},{14,12},{16,18},{18,... | collective-permute-start | bytes 1769480 | tf_op jit(solution)/shard_map/ppermute | solution.py:254
  161.6 130.1 %collective-permute-start.33 = (bf16[2,2,2,1,48,2048]{5,4,3,2,1,0:T(8,128)(2,1)}, bf16[2,2,2,1,48,2048]{5,4,3,2,1,0:T(8,128)(2,1)}, u32[]{:S(2)}, u32[]{:S(2)}) collective-permute-start(bf16[2,2,2,1,48,2048]{5,4,3,2,1,0:T(8,128)(2,1)} %constant_dynamic-slice_fusion.14), channel_id=1, source_target_pairs={{0,2},{2,0},{4,6},{6,4},{8,10},{10,8},{12,14},{14,12},{16,18},{18,... | collective-permute-start | bytes 4718600 | tf_op jit(solution)/shard_map/ppermute | solution.py:254
  200.2 8.7 %collective-permute-start.29 = (bf16[2,2,2,1,48,384]{5,4,3,2,1,0:T(8,128)(2,1)S(1)}, bf16[2,2,2,1,48,384]{5,4,3,2,1,0:T(8,128)(2,1)S(1)}, u32[]{:S(2)}, u32[]{:S(2)}) collective-permute-start(bf16[2,2,2,1,48,384]{5,4,3,2,1,0:T(8,128)(2,1)S(1)} %constant_dynamic-slice_fusion.18), channel_id=1, source_target_pairs={{0,1},{1,0},{2,3},{3,2},{4,5},{5,4},{6,7},{7,6},{8,9},{9,8},{10,11... | collective-permute-start | bytes 884744 | tf_op jit(solution)/shard_map/ppermute | solution.py:258
  203.2 29.0 %copy-start.1 = (f32[1024,768]{1,0:T(8,128)}, f32[1024,768]{1,0:T(8,128)S(1)}, u32[]{:S(2)}) copy-start(f32[1024,768]{1,0:T(8,128)S(1)} %fusion.18) | copy-start | bytes 9437188
  209.1 5.2 %collective-permute-start.30 = (bf16[2,2,1,1,48,384]{5,4,3,2,1,0:T(8,128)(2,1)S(1)}, bf16[2,2,1,1,48,384]{5,4,3,2,1,0:T(8,128)(2,1)S(1)}, u32[]{:S(2)}, u32[]{:S(2)}) collective-permute-start(bf16[2,2,1,1,48,384]{5,4,3,2,1,0:T(8,128)(2,1)S(1)} %constant_dynamic-slice_fusion.17), channel_id=1, source_target_pairs={{0,4},{2,6},{4,0},{6,2},{8,12},{10,14},{12,8},{14,10},{16,20},{18,... | collective-permute-start | bytes 442376 | tf_op jit(solution)/shard_map/ppermute | solution.py:254
  213.1 7.7 %copy-start.8 = (bf16[768,1152]{1,0:T(8,128)(2,1)}, bf16[768,1152]{1,0:T(8,128)(2,1)S(1)}, u32[]{:S(2)}) copy-start(bf16[768,1152]{1,0:T(8,128)(2,1)S(1)} %convolution_convert_fusion.4) | copy-start | bytes 5308420
  214.4 4.4 %collective-permute-start.31 = (bf16[2,1,1,1,48,384]{5,4,3,2,1,0:T(8,128)(2,1)S(1)}, bf16[2,1,1,1,48,384]{5,4,3,2,1,0:T(8,128)(2,1)S(1)}, u32[]{:S(2)}, u32[]{:S(2)}) collective-permute-start(bf16[2,1,1,1,48,384]{5,4,3,2,1,0:T(8,128)(2,1)S(1)} %constant_dynamic-slice_fusion.16), channel_id=1, source_target_pairs={{0,8},{2,10},{4,12},{6,14},{8,0},{10,2},{12,4},{14,6},{16,24},{18,... | collective-permute-start | bytes 221192 | tf_op jit(solution)/shard_map/ppermute | solution.py:254
  215.3 16.9 %collective-permute-start.23 = (bf16[512,768]{1,0:T(8,128)(2,1)S(1)}, bf16[512,768]{1,0:T(8,128)(2,1)S(1)}, u32[]{:S(2)}, u32[]{:S(2)}) collective-permute-start(bf16[512,768]{1,0:T(8,128)(2,1)S(1)} %dynamic-slice_convert_fusion), channel_id=1, source_target_pairs={{0,1},{1,0},{2,3},{3,2},{4,5},{5,4},{6,7},{7,6},{8,9},{9,8},{10,11... | collective-permute-start | bytes 2359304 | tf_op jit(solution)/shard_map/ppermute | solution.py:258
  218.8 4.9 %collective-permute-start.32 = (bf16[1,1,1,1,48,384]{5,4,3,2,1,0:T(8,128)(2,1)S(1)}, bf16[1,1,1,1,48,384]{5,4,3,2,1,0:T(8,128)(2,1)S(1)}, u32[]{:S(2)}, u32[]{:S(2)}) collective-permute-start(bf16[1,1,1,1,48,384]{5,4,3,2,1,0:T(8,128)(2,1)S(1)} %constant_dynamic-slice_fusion.15), channel_id=1, source_target_pairs={{0,16},{2,18},{4,20},{6,22},{8,24},{10,26},{12,28},{14,30},{16,0},... | collective-permute-start | bytes 110600 | tf_op jit(solution)/shard_map/ppermute | solution.py:254
  220.7 12.3 %copy-start.19 = (f32[768]{0:T(1024)S(1)}, f32[768]{0:T(1024)}, u32[]{:S(2)}) copy-start(f32[768]{0:T(1024)} %get-tuple-element.19) | copy-start | bytes 9220
  223.8 51.6 %collective-permute-start.24 = (bf16[2,2,2,1,48,1152]{5,4,3,2,1,0:T(8,128)(2,1)}, bf16[2,2,2,1,48,1152]{5,4,3,2,1,0:T(8,128)(2,1)}, u32[]{:S(2)}, u32[]{:S(2)}) collective-permute-start(bf16[2,2,2,1,48,1152]{5,4,3,2,1,0:T(8,128)(2,1)} %constant_dynamic-slice_fusion.23), channel_id=1, source_target_pairs={{0,2},{2,0},{4,6},{6,4},{8,10},{10,8},{12,14},{14,12},{16,18},{18,... | collective-permute-start | bytes 2654216 | tf_op jit(solution)/shard_map/ppermute | solution.py:254
  272.4 3.0 copy-start.9
  275.4 4.2 %copy-start.7 = (bf16[2048,768]{1,0:T(8,128)(2,1)S(1)}, bf16[2048,768]{1,0:T(8,128)(2,1)}, u32[]{:S(2)}) copy-start(bf16[2048,768]{1,0:T(8,128)(2,1)} %copy-done.6) | copy-start | bytes 9437188
  277.0 13.7 %collective-permute-start.25 = (bf16[2,2,1,1,48,1152]{5,4,3,2,1,0:T(8,128)(2,1)S(1)}, bf16[2,2,1,1,48,1152]{5,4,3,2,1,0:T(8,128)(2,1)S(1)}, u32[]{:S(2)}, u32[]{:S(2)}) collective-permute-start(bf16[2,2,1,1,48,1152]{5,4,3,2,1,0:T(8,128)(2,1)S(1)} %constant_dynamic-slice_fusion.22), channel_id=1, source_target_pairs={{0,4},{2,6},{4,0},{6,2},{8,12},{10,14},{12,8},{14,10},{16,20},{18,... | collective-permute-start | bytes 1327112 | tf_op jit(solution)/shard_map/ppermute | solution.py:254
  281.6 25.9 %collective-permute-start.44 = (bf16[2,2,1,1,128,768]{5,4,3,2,1,0:T(8,128)(2,1)S(1)}, bf16[2,2,1,1,128,768]{5,4,3,2,1,0:T(8,128)(2,1)S(1)}, u32[]{:S(2)}, u32[]{:S(2)}) collective-permute-start(bf16[2,2,1,1,128,768]{5,4,3,2,1,0:T(8,128)(2,1)S(1)} %constant_dynamic-slice_fusion.3), channel_id=1, source_target_pairs={{0,4},{2,6},{4,0},{6,2},{8,12},{10,14},{12,8},{14,10},{16,20},{18,... | collective-permute-start | bytes 2359304 | tf_op jit(solution)/shard_map/ppermute | solution.py:254
  284.0 7.6 %copy-start.3 = (bf16[768,2048]{1,0:T(8,128)(2,1)S(1)}, bf16[768,2048]{1,0:T(8,128)(2,1)}, u32[]{:S(2)}) copy-start(bf16[768,2048]{1,0:T(8,128)(2,1)} %copy-done.2) | copy-start | bytes 9437188
  284.1 24.5 %collective-permute-start.39 = (bf16[2,2,2,1,48,1024]{5,4,3,2,1,0:T(8,128)(2,1)S(1)}, bf16[2,2,2,1,48,1024]{5,4,3,2,1,0:T(8,128)(2,1)S(1)}, u32[]{:S(2)}, u32[]{:S(2)}) collective-permute-start(bf16[2,2,2,1,48,1024]{5,4,3,2,1,0:T(8,128)(2,1)S(1)} %constant_dynamic-slice_fusion.8), channel_id=1, source_target_pairs={{0,1},{1,0},{2,3},{3,2},{4,5},{5,4},{6,7},{7,6},{8,9},{9,8},{10,11... | collective-permute-start | bytes 2359304 | tf_op jit(solution)/shard_map/ppermute | solution.py:258
  290.8 6.7 %collective-permute-start.26 = (bf16[2,1,1,1,48,1152]{5,4,3,2,1,0:T(8,128)(2,1)S(1)}, bf16[2,1,1,1,48,1152]{5,4,3,2,1,0:T(8,128)(2,1)S(1)}, u32[]{:S(2)}, u32[]{:S(2)}) collective-permute-start(bf16[2,1,1,1,48,1152]{5,4,3,2,1,0:T(8,128)(2,1)S(1)} %constant_dynamic-slice_fusion.21), channel_id=1, source_target_pairs={{0,8},{2,10},{4,12},{6,14},{8,0},{10,2},{12,4},{14,6},{16,24},{18,... | collective-permute-start | bytes 663560 | tf_op jit(solution)/shard_map/ppermute | solution.py:254
  297.6 6.9 %collective-permute-start.27 = (bf16[1,1,1,1,48,1152]{5,4,3,2,1,0:T(8,128)(2,1)S(1)}, bf16[1,1,1,1,48,1152]{5,4,3,2,1,0:T(8,128)(2,1)S(1)}, u32[]{:S(2)}, u32[]{:S(2)}) collective-permute-start(bf16[1,1,1,1,48,1152]{5,4,3,2,1,0:T(8,128)(2,1)S(1)} %constant_dynamic-slice_fusion.20), channel_id=1, source_target_pairs={{0,16},{2,18},{4,20},{6,22},{8,24},{10,26},{12,28},{14,30},{16,0},... | collective-permute-start | bytes 331784 | tf_op jit(solution)/shard_map/ppermute | solution.py:254
  298.3 26.1 %collective-permute-start.34 = (bf16[2,2,1,1,48,2048]{5,4,3,2,1,0:T(8,128)(2,1)S(1)}, bf16[2,2,1,1,48,2048]{5,4,3,2,1,0:T(8,128)(2,1)S(1)}, u32[]{:S(2)}, u32[]{:S(2)}) collective-permute-start(bf16[2,2,1,1,48,2048]{5,4,3,2,1,0:T(8,128)(2,1)S(1)} %constant_dynamic-slice_fusion.13), channel_id=1, source_target_pairs={{0,4},{2,6},{4,0},{6,2},{8,12},{10,14},{12,8},{14,10},{16,20},{18,... | collective-permute-start | bytes 2359304 | tf_op jit(solution)/shard_map/ppermute | solution.py:254
  307.8 18.7 %collective-permute-start.45 = (bf16[2,1,1,1,128,768]{5,4,3,2,1,0:T(8,128)(2,1)S(1)}, bf16[2,1,1,1,128,768]{5,4,3,2,1,0:T(8,128)(2,1)S(1)}, u32[]{:S(2)}, u32[]{:S(2)}) collective-permute-start(bf16[2,1,1,1,128,768]{5,4,3,2,1,0:T(8,128)(2,1)S(1)} %constant_dynamic-slice_fusion.2), channel_id=1, source_target_pairs={{0,8},{2,10},{4,12},{6,14},{8,0},{10,2},{12,4},{14,6},{16,24},{18,... | collective-permute-start | bytes 1179656 | tf_op jit(solution)/shard_map/ppermute | solution.py:254
  309.0 22.2 %collective-permute-start.40 = (bf16[2,2,1,1,48,1024]{5,4,3,2,1,0:T(8,128)(2,1)S(1)}, bf16[2,2,1,1,48,1024]{5,4,3,2,1,0:T(8,128)(2,1)S(1)}, u32[]{:S(2)}, u32[]{:S(2)}) collective-permute-start(bf16[2,2,1,1,48,1024]{5,4,3,2,1,0:T(8,128)(2,1)S(1)} %constant_dynamic-slice_fusion.7), channel_id=1, source_target_pairs={{0,4},{2,6},{4,0},{6,2},{8,12},{10,14},{12,8},{14,10},{16,20},{18,... | collective-permute-start | bytes 1179656 | tf_op jit(solution)/shard_map/ppermute | solution.py:254
  324.7 7.9 %collective-permute-start.35 = (bf16[2,2,1,1,48,1024]{5,4,3,2,1,0:T(8,128)(2,1)S(1)}, bf16[2,2,1,1,48,1024]{5,4,3,2,1,0:T(8,128)(2,1)S(1)}, u32[]{:S(2)}, u32[]{:S(2)}) collective-permute-start(bf16[2,2,1,1,48,1024]{5,4,3,2,1,0:T(8,128)(2,1)S(1)} %constant_dynamic-slice_fusion.12), channel_id=1, source_target_pairs={{0,1},{1,0},{2,3},{3,2},{4,5},{5,4},{6,7},{7,6},{8,9},{9,8},{10,11... | collective-permute-start | bytes 1179656 | tf_op jit(solution)/shard_map/ppermute | solution.py:258
  326.6 8.8 %collective-permute-start.46 = (bf16[1,1,1,1,128,768]{5,4,3,2,1,0:T(8,128)(2,1)S(1)}, bf16[1,1,1,1,128,768]{5,4,3,2,1,0:T(8,128)(2,1)S(1)}, u32[]{:S(2)}, u32[]{:S(2)}) collective-permute-start(bf16[1,1,1,1,128,768]{5,4,3,2,1,0:T(8,128)(2,1)S(1)} %constant_dynamic-slice_fusion.1), channel_id=1, source_target_pairs={{0,16},{2,18},{4,20},{6,22},{8,24},{10,26},{12,28},{14,30},{16,0},... | collective-permute-start | bytes 589832 | tf_op jit(solution)/shard_map/ppermute | solution.py:254
  331.3 8.4 %collective-permute-start.41 = (bf16[2,1,1,1,48,1024]{5,4,3,2,1,0:T(8,128)(2,1)S(1)}, bf16[2,1,1,1,48,1024]{5,4,3,2,1,0:T(8,128)(2,1)S(1)}, u32[]{:S(2)}, u32[]{:S(2)}) collective-permute-start(bf16[2,1,1,1,48,1024]{5,4,3,2,1,0:T(8,128)(2,1)S(1)} %constant_dynamic-slice_fusion.6), channel_id=1, source_target_pairs={{0,8},{2,10},{4,12},{6,14},{8,0},{10,2},{12,4},{14,6},{16,24},{18,... | collective-permute-start | bytes 589832 | tf_op jit(solution)/shard_map/ppermute | solution.py:254
  332.8 11.0 %collective-permute-start.36 = (bf16[2,1,1,1,48,1024]{5,4,3,2,1,0:T(8,128)(2,1)S(1)}, bf16[2,1,1,1,48,1024]{5,4,3,2,1,0:T(8,128)(2,1)S(1)}, u32[]{:S(2)}, u32[]{:S(2)}) collective-permute-start(bf16[2,1,1,1,48,1024]{5,4,3,2,1,0:T(8,128)(2,1)S(1)} %constant_dynamic-slice_fusion.11), channel_id=1, source_target_pairs={{0,8},{2,10},{4,12},{6,14},{8,0},{10,2},{12,4},{14,6},{16,24},{18,... | collective-permute-start | bytes 589832 | tf_op jit(solution)/shard_map/ppermute | solution.py:254
  335.6 8.6 %collective-permute-start.47 = (bf16[1,1,1,1,128,384]{5,4,3,2,1,0:T(8,128)(2,1)S(1)}, bf16[1,1,1,1,128,384]{5,4,3,2,1,0:T(8,128)(2,1)S(1)}, u32[]{:S(2)}, u32[]{:S(2)}) collective-permute-start(bf16[1,1,1,1,128,384]{5,4,3,2,1,0:T(8,128)(2,1)S(1)} %constant_dynamic-slice_fusion), channel_id=1, source_target_pairs={{0,1},{1,0},{2,3},{3,2},{4,5},{5,4},{6,7},{7,6},{8,9},{9,8},{10,11... | collective-permute-start | bytes 294920 | tf_op jit(solution)/shard_map/ppermute | solution.py:258
  339.8 7.1 %collective-permute-start.42 = (bf16[1,1,1,1,48,1024]{5,4,3,2,1,0:T(8,128)(2,1)S(1)}, bf16[1,1,1,1,48,1024]{5,4,3,2,1,0:T(8,128)(2,1)S(1)}, u32[]{:S(2)}, u32[]{:S(2)}) collective-permute-start(bf16[1,1,1,1,48,1024]{5,4,3,2,1,0:T(8,128)(2,1)S(1)} %constant_dynamic-slice_fusion.5), channel_id=1, source_target_pairs={{0,16},{2,18},{4,20},{6,22},{8,24},{10,26},{12,28},{14,30},{16,0},... | collective-permute-start | bytes 294920 | tf_op jit(solution)/shard_map/ppermute | solution.py:254
  343.8 6.2 %collective-permute-start.37 = (bf16[1,1,1,1,48,1024]{5,4,3,2,1,0:T(8,128)(2,1)S(1)}, bf16[1,1,1,1,48,1024]{5,4,3,2,1,0:T(8,128)(2,1)S(1)}, u32[]{:S(2)}, u32[]{:S(2)}) collective-permute-start(bf16[1,1,1,1,48,1024]{5,4,3,2,1,0:T(8,128)(2,1)S(1)} %constant_dynamic-slice_fusion.10), channel_id=1, source_target_pairs={{0,16},{2,18},{4,20},{6,22},{8,24},{10,26},{12,28},{14,30},{16,0},... | collective-permute-start | bytes 294920 | tf_op jit(solution)/shard_map/ppermute | solution.py:254
  (6 other events, 8.4 us)

commit v2 on v1

--- a/solution.py
+++ b/solution.py
@@ -267,6 +267,14 @@
     return lax.dynamic_update_slice_in_dim(whole, other, (1 - later) * width, axis)
 
 
+def add(kept, other):
+    return (kept.astype(jnp.float32) + other.astype(jnp.float32)).astype(jnp.bfloat16)
+
+
+def after(*values):
+    return lax.optimization_barrier(values)
+
+
 class Place:
     def __init__(self, items):
         self.items = items
@@ -277,38 +285,41 @@
     def bit(self, level):
         return (self.index >> (self.levels - 1 - level)) & 1
 
-    def gather(self, shard, order):
-        rows, columns = shard.shape
-        whole = shard.reshape((1,) * self.levels + (rows, columns))
+    def shaped(self, shard):
+        return shard.reshape((1,) * self.levels + shard.shape)
+
+    def flat(self, whole):
+        return whole.reshape(-1, whole.shape[-1])
+
+    def send(self, whole, step):
+        if step == "blk":
+            return swap_blocks(whole)
+        return swap_items(whole, self.items, 1 << (self.levels - 1 - step))
+
+    def meet(self, whole, other, step):
+        if step == "blk":
+            return join(whole, other, self.levels + 1, self.block)
+        return join(whole, other, step, self.bit(step))
+
+    def gather(self, whole, order):
         for step in order:
-            if step == "blk":
-                whole = join(whole, swap_blocks(whole), self.levels + 1, self.block)
-            else:
-                other = swap_items(whole, self.items, 1 << (self.levels - 1 - step))
-                whole = join(whole, other, step, self.bit(step))
-        return whole.reshape(-1, whole.shape[-1])
-
-    def scatter(self, whole, rows, order):
-        part = whole.reshape((2,) * self.levels + (rows, whole.shape[-1]))
+            whole = self.meet(whole, self.send(whole, step), step)
+        return whole
+
+    def part_of(self, whole, rows):
+        return whole.reshape((2,) * self.levels + (rows, whole.shape[-1]))
+
+    def halves(self, part, step):
+        axis, mine = (self.levels + 1, self.block) if step == "blk" else (step, self.bit(step))
+        width = part.shape[axis] // 2
+        kept = lax.dynamic_slice_in_dim(part, mine * width, width, axis)
+        sent = lax.dynamic_slice_in_dim(part, (1 - mine) * width, width, axis)
+        return kept, self.send(sent, step)
+
+    def scatter(self, part, order):
         for step in order:
-            if step == "blk":
-                axis, mine = self.levels + 1, self.block
-            else:
-                axis, mine = step, self.bit(step)
-            width = part.shape[axis] // 2
-            kept = lax.dynamic_slice_in_dim(part, mine * width, width, axis)
-            sent = lax.dynamic_slice_in_dim(part, (1 - mine) * width, width, axis)
-            if step == "blk":
-                other = swap_blocks(sent)
-            else:
-                other = swap_items(sent, self.items, 1 << (self.levels - 1 - step))
-            part = (kept.astype(jnp.float32) + other.astype(jnp.float32)).astype(jnp.bfloat16)
-        return part.reshape(rows, -1).astype(jnp.float32)
-
-    def total(self, values):
-        for level in range(self.levels):
-            values = values + swap_items(values, self.items, 1 << level)
-        return values + swap_blocks(values)
+            part = add(*self.halves(part, step))
+        return part
 
 
 def own_lanes(values, head):
@@ -344,21 +355,22 @@
     out_ref[...] = total.astype(jnp.bfloat16)
 
 
-def attend(count, qkv, rows=256):
-    length, width = qkv.shape[0], qkv.shape[1] // 3
-    groups = width // 128
+def attend(count, qkv, first, some, rows=256):
+    length, groups = qkv.shape[0], qkv.shape[1] // 384
+    width = some * 128
     return pl.pallas_call(
         attend_kernel,
-        grid=(groups, length // rows),
+        grid=(some, length // rows),
         in_specs=[
             pl.BlockSpec(memory_space=pltpu.SMEM),
-            pl.BlockSpec((rows, 128), lambda g, r: (r, g)),
-            pl.BlockSpec((length, 128), lambda g, r: (0, groups + g)),
-            pl.BlockSpec((length, 128), lambda g, r: (0, 2 * groups + g)),
+            pl.BlockSpec((rows, 128), lambda g, r: (r, first + g)),
+            pl.BlockSpec((length, 128), lambda g, r: (0, groups + first + g)),
+            pl.BlockSpec((length, 128), lambda g, r: (0, 2 * groups + first + g)),
         ],
         out_specs=pl.BlockSpec((rows, 128), lambda g, r: (r, g)),
         out_shape=jax.ShapeDtypeStruct((length, width), jnp.bfloat16),
-        compiler_params=pltpu.CompilerParams(vmem_limit_bytes=40 << 20),
+        compiler_params=pltpu.CompilerParams(vmem_limit_bytes=16 << 20),
+        cost_estimate=pl.CostEstimate(flops=16 * length * length * width, bytes_accessed=8 * length * width, transcendentals=length * length * width // HEAD),
         name="attend",
     )(count, qkv, qkv, qkv)
 
@@ -398,28 +410,28 @@
         dv_ref[...] = dv_sum[...].astype(jnp.bfloat16)
 
 
-def attend_back(count, qkv, grad, rows=256):
-    length, width = grad.shape
-    groups = width // 128
-    shape = jax.ShapeDtypeStruct((length, width), jnp.bfloat16)
+def attend_back(count, qkv, grad, group, rows=256):
+    length, groups = qkv.shape[0], qkv.shape[1] // 384
+    shape = jax.ShapeDtypeStruct((length, 128), jnp.bfloat16)
     return pl.pallas_call(
         attend_back_kernel,
-        grid=(groups, length // rows),
+        grid=(1, length // rows),
         in_specs=[
             pl.BlockSpec(memory_space=pltpu.SMEM),
-            pl.BlockSpec((rows, 128), lambda g, r: (r, g)),
-            pl.BlockSpec((length, 128), lambda g, r: (0, groups + g)),
-            pl.BlockSpec((length, 128), lambda g, r: (0, 2 * groups + g)),
-            pl.BlockSpec((rows, 128), lambda g, r: (r, g)),
+            pl.BlockSpec((rows, 128), lambda g, r: (r, group)),
+            pl.BlockSpec((length, 128), lambda g, r: (0, groups + group)),
+            pl.BlockSpec((length, 128), lambda g, r: (0, 2 * groups + group)),
+            pl.BlockSpec((rows, 128), lambda g, r: (r, group)),
         ],
         out_specs=[
-            pl.BlockSpec((rows, 128), lambda g, r: (r, g)),
-            pl.BlockSpec((length, 128), lambda g, r: (0, g)),
-            pl.BlockSpec((length, 128), lambda g, r: (0, g)),
+            pl.BlockSpec((rows, 128), lambda g, r: (r, 0)),
+            pl.BlockSpec((length, 128), lambda g, r: (0, 0)),
+            pl.BlockSpec((length, 128), lambda g, r: (0, 0)),
         ],
         out_shape=[shape, shape, shape],
         scratch_shapes=[pltpu.VMEM((length, 128), jnp.float32), pltpu.VMEM((length, 128), jnp.float32)],
-        compiler_params=pltpu.CompilerParams(vmem_limit_bytes=40 << 20),
+        compiler_params=pltpu.CompilerParams(vmem_limit_bytes=16 << 20),
+        cost_estimate=pl.CostEstimate(flops=5000 * length * length, bytes_accessed=14 * length * 128, transcendentals=2 * length * length),
         name="attend_back",
     )(count, qkv, qkv, qkv, grad)
 
@@ -449,31 +461,64 @@
     own_rows, own_cot = patches[0], cotangent[0]
     shard_rows, down_rows = w_query.shape[0], w_down.shape[0]
 
-    all_rows = join(own_rows, swap_blocks(own_rows), 0, block)
-    attn_weights = place.gather(
-        jnp.concatenate([w_query, w_key, w_value, w_out], 1), far + [levels - 2, levels - 1]
-    )
-    w_qkv, out_half = attn_weights[:, : 3 * half], attn_weights[:, 3 * half :]
-    full_gate = place.gather(w_gate, far + ["blk", levels - 2, levels - 1])
-    full_up = place.gather(w_up, far + [levels - 2, "blk", levels - 1])
-    full_down = place.gather(w_down, ["blk"] + far + [levels - 2, levels - 1])
-    full_out = join(out_half, swap_blocks(out_half), 1, block)
-
+    y, core = levels - 2, levels - 1
+    groups = half // 128
+    other_rows = swap_blocks(own_rows)
+    w_qkv = place.shaped(jnp.concatenate([w_query, w_key, w_value], 1))
+    gate, up, down, out = [place.shaped(shard) for shard in (w_gate, w_up, w_down, w_out)]
+
+    def advance(held, steps):
+        moved = [whole if step is None else place.send(whole, step) for whole, step in zip(held, steps)]
+        moved = after(*moved)
+        return [
+            other if step is None else place.meet(whole, other, step)
+            for whole, other, step in zip(held, moved, steps)
+        ]
+
+    w_qkv, down = advance([w_qkv, down], [far[0], "blk"])
+    w_qkv, gate, up, down = advance([w_qkv, gate, up, down], [far[1], far[0], far[0], y])
+    w_qkv, gate, up, out, down = advance([w_qkv, gate, up, out, down], [y, far[1], far[1], far[0], None])
+    for step in far[2:]:
+        w_qkv, gate, up = advance([w_qkv, gate, up], [step] * 3)
+    w_qkv, out, down = advance([w_qkv, out, down], [core, far[1], None])
+    w_qkv = place.flat(w_qkv)
+
+    sent = place.send(gate, "blk"), place.send(up, y), place.send(down, far[0]), place.send(out, "blk")
+    all_rows = join(own_rows, other_rows, 0, block)
     all_normed = rms_norm(all_rows.astype(jnp.float32), norm_attn).astype(jnp.bfloat16)
     qkv = dot_nn(all_normed, w_qkv).astype(jnp.bfloat16)
-    attended_heads = attend(count, qkv)
+    early = attend(count, qkv, 0, groups - 1)
+    early, qkv_late, sent = after(early, qkv, sent)
+    gate = place.meet(gate, sent[0], "blk")
+    up = place.meet(up, sent[1], y)
+    down = place.meet(down, sent[2], far[0])
+    out = place.meet(out, sent[3], "blk")
 
     def exchange_rows(values):
         kept = lax.dynamic_slice_in_dim(values, block * row_count, row_count, 0)
         sent = lax.dynamic_slice_in_dim(values, (1 - block) * row_count, row_count, 0)
-        return join(kept, swap_blocks(sent), 1, block)
-
-    def exchange_heads(values):
-        kept = lax.dynamic_slice_in_dim(values, block * half, half, 1)
-        sent = lax.dynamic_slice_in_dim(values, (1 - block) * half, half, 1)
-        return join(kept, swap_blocks(sent), 0, block)
-
-    attended = exchange_rows(attended_heads)
+        return kept, swap_blocks(sent)
+
+    early_kept, early_other = exchange_rows(early)
+    sent = place.send(out, y), place.send(gate, y), place.send(down, far[1])
+    late = attend(count, qkv_late, groups - 1, 1)
+    early_other, up = after(early_other, up)
+    sent += (place.send(up, "blk"),)
+    late_kept, late_other = exchange_rows(late)
+    late_other, sent = after(late_other, sent)
+    out = place.meet(out, sent[0], y)
+    gate = place.meet(gate, sent[1], y)
+    down = place.meet(down, sent[2], far[1])
+    up = place.meet(up, sent[3], "blk")
+    out, gate, up, down = [place.gather(whole, far[2:]) for whole in (out, gate, up, down)]
+    full_out = place.flat(place.gather(out, [core]))
+    full_gate = place.flat(place.gather(gate, [core]))
+    full_up = place.flat(place.gather(up, [core]))
+    full_down = place.flat(place.gather(down, [core]))
+    attended = join(
+        jnp.concatenate([early_kept, late_kept], 1), jnp.concatenate([early_other, late_other], 1), 1, block
+    )
+    near = far[::-1]
     patch_rows = own_rows.astype(jnp.float32)
     middle = patch_rows + dot_nn(attended, full_out)
     normed_mlp = rms_norm(middle, norm_mlp).astype(jnp.bfloat16)
@@ -483,37 +528,87 @@
     hidden = (activated * upward).astype(jnp.bfloat16)
     output = (middle + dot_nn(hidden, full_down)).astype(jnp.bfloat16)
     grad_down = dot_tn(hidden, own_cot).astype(jnp.bfloat16)
+    moving = place.halves(place.part_of(grad_down, down_rows), core)
     grad_hidden = dot_nt(own_cot, full_down)
     unused_gelu, gelu_back = jax.vjp(lambda inner: jax.nn.gelu(inner, approximate=True), gate_in)
     grad_gate_in = gelu_back(grad_hidden * upward)[0].astype(jnp.bfloat16)
     grad_upward = (grad_hidden * activated).astype(jnp.bfloat16)
-    grad_gate = dot_tn(normed_mlp, grad_gate_in).astype(jnp.bfloat16)
-    grad_up = dot_tn(normed_mlp, grad_upward).astype(jnp.bfloat16)
     grad_normed_mlp = dot_nt(grad_gate_in, full_gate) + dot_nt(grad_upward, full_up)
+    grad_normed_mlp, moving = after(grad_normed_mlp, moving)
+    moving = place.halves(add(*moving), near[0])
     unused_norm, second_back = jax.vjp(rms_norm, middle, norm_mlp)
     grad_middle_part, gain_mlp = second_back(grad_normed_mlp)
     grad_middle = own_cot.astype(jnp.float32) + grad_middle_part
     branch_grad = grad_middle.astype(jnp.bfloat16)
     grad_attended = dot_nt(branch_grad, full_out).astype(jnp.bfloat16)
+    heads_kept = lax.dynamic_slice_in_dim(grad_attended, block * half, half, 1)
+    heads_sent = lax.dynamic_slice_in_dim(grad_attended, (1 - block) * half, half, 1)
+    heads_other = swap_blocks(heads_sent)
+    normed_mlp, attended, heads_sent = after(normed_mlp, attended, heads_sent)
+    grad_gate = dot_tn(normed_mlp, grad_gate_in).astype(jnp.bfloat16)
+    grad_up = dot_tn(normed_mlp, grad_upward).astype(jnp.bfloat16)
     grad_out = dot_tn(attended, branch_grad).astype(jnp.bfloat16)
-    grad_heads = exchange_heads(grad_attended)
-    grad_qkv = jnp.concatenate(attend_back(count, qkv, grad_heads), 1)
+    cores = [place.halves(place.part_of(grad, shard_rows), core) for grad in (grad_gate, grad_up, grad_out)]
+    heads_other, grad_gate, grad_up, grad_out = after(heads_other, grad_gate, grad_up, grad_out)
+    grad_heads = join(heads_kept, heads_other, 0, block)
+    part_gate, part_up, part_out = [add(*pair) for pair in cores]
+
+    wide = place.halves(part_gate, y), place.halves(part_up, "blk")
+    backs = attend_back(count, qkv, grad_heads, 0)
+    backs, grad_heads, moving = after(backs, grad_heads, moving)
+    backs = [backs]
+    moving = place.halves(add(*moving), near[1])
+    for group in range(1, groups - 1):
+        backs.append(attend_back(count, qkv, grad_heads, group))
+    backs, grad_heads, wide = after(backs, grad_heads, wide)
+    part_gate, part_up = [add(*pair) for pair in wide]
+    wide = place.halves(part_gate, "blk"), place.halves(part_up, y), place.halves(part_out, y)
+    last = attend_back(count, qkv, grad_heads, groups - 1)
+    last, wide, moving = after(last, wide, moving)
+    backs = backs + [last]
+    part_gate, part_up, part_out = [add(*pair) for pair in wide]
+    part_down = add(*moving)
+    part_gate = jnp.concatenate([part_gate, part_up], -1)
+
+    grad_qkv = jnp.concatenate([back[kind] for kind in range(3) for back in backs], 1)
+    grad_all_normed = dot_nt(grad_qkv, w_qkv)
+    unused_all, gain_back = jax.vjp(lambda gain: rms_norm(all_rows.astype(jnp.float32), gain), norm_attn)
+    gains = jnp.stack([gain_back(grad_all_normed)[0], gain_mlp])
+    gains = gains + swap_blocks(gains)
+    rows_kept = lax.dynamic_slice_in_dim(grad_all_normed, block * row_count, row_count, 0)
+    rows_sent = lax.dynamic_slice_in_dim(grad_all_normed, (1 - block) * row_count, row_count, 0)
+    rows_sent, gains = after(rows_sent.astype(jnp.bfloat16), gains)
+    rows_other = swap_blocks(rows_sent)
     grad_w_qkv = dot_tn(all_normed, grad_qkv).astype(jnp.bfloat16)
-    grad_all_normed = dot_nt(grad_qkv, w_qkv)
-    kept = lax.dynamic_slice_in_dim(grad_all_normed, block * row_count, row_count, 0)
-    sent = lax.dynamic_slice_in_dim(grad_all_normed, (1 - block) * row_count, row_count, 0)
-    grad_normed = kept + swap_blocks(sent.astype(jnp.bfloat16)).astype(jnp.float32)
+    moving = place.halves(place.part_of(grad_w_qkv, shard_rows), core)
+    other_gains = place.send(gains, core)
+    moving, other_gains = after(moving, other_gains)
+    part_qkv, gains = add(*moving), gains + other_gains
+
+    moving = place.halves(part_qkv, y), place.halves(part_gate, near[0])
+    other_gains = place.send(gains, y)
+    rows_other, moving, other_gains = after(rows_other, moving, other_gains)
+    part_qkv, part_gate = [add(*pair) for pair in moving]
+    gains = gains + other_gains
+
+    moving = place.halves(part_qkv, near[0]), place.halves(part_gate, near[1]), place.halves(part_out, "blk"), place.halves(part_down, y)
+    other_gains = place.send(gains, near[0])
+    moving, other_gains = after(moving, other_gains)
+    part_qkv, part_gate, part_out, part_down = [add(*pair) for pair in moving]
+    gains = gains + other_gains
+    for step in near[1:]:
+        gains = gains + place.send(gains, step)
+
+    grad_normed = rows_kept + rows_other.astype(jnp.float32)
     unused_first, first_back = jax.vjp(rms_norm, patch_rows, norm_attn)
-    grad_rows_part, gain_attn = first_back(grad_normed)
+    grad_rows_part, unused_gain = first_back(grad_normed)
     grad_patches = (grad_middle + grad_rows_part).astype(jnp.bfloat16)
 
-    near = far[::-1]
-    shard_down = place.scatter(grad_down, down_rows, [levels - 1, levels - 2] + near + ["blk"])
-    shard_gate = place.scatter(grad_gate, shard_rows, [levels - 1, levels - 2, "blk"] + near)
-    shard_up = place.scatter(grad_up, shard_rows, [levels - 1, "blk", levels - 2] + near)
-    shard_out = place.scatter(grad_out, shard_rows, [levels - 1, "blk", levels - 2] + near)
-    shard_qkv = place.scatter(grad_w_qkv, shard_rows, [levels - 1, levels - 2] + near)
-    gains = lax.psum((gain_attn, gain_mlp), ("items", "blk"))
+    shard_qkv = place.scatter(part_qkv, near[1:]).reshape(shard_rows, -1).astype(jnp.float32)
+    shard_down = place.scatter(part_down, ["blk"] + near[2:]).reshape(down_rows, half).astype(jnp.float32)
+    shard_out = place.scatter(part_out, near).reshape(shard_rows, half).astype(jnp.float32)
+    shard_gate = place.scatter(part_gate, near[2:]).reshape(shard_rows, -1).astype(jnp.float32)
+    inner = shard_gate.shape[1] // 2
     return (
         output[None],
         grad_patches[None],
@@ -523,8 +618,8 @@
         shard_qkv[:, 2 * half :],
         shard_out,
         gains[1],
-        shard_gate,
-        shard_up,
+        shard_gate[:, :inner],
+        shard_gate[:, inner:],
         shard_down,
     )
 

time: 357 us -> 256 us (0.72)
  waiting for transfers between devices: 137 us -> 78.7 us
  blocking collectives: 39.4 us -> 0 us
  starting transfers between devices: 49.7 us -> 60.8 us
  other arithmetic: 18.8 us -> 10.6 us
  matrix products: 38.4 us -> 33.1 us
    ppermute x36 -> x42, waiting for transfers between devices: 97.7 us -> 41.1 us  [swap_items(): lax.ppermute(values, 'items', [(place, place ^ bit) for place in range(it...]
    psum x1 -> x0, blocking collectives: 39.4 us -> none  [by_heads(): gains = lax.psum((gain_attn, gain_mlp), ('items', 'blk'))]
    ppermute x36 -> x42, starting transfers between devices: 36.8 us -> 46.1 us  [swap_items(): lax.ppermute(values, 'items', [(place, place ^ bit) for place in range(it...]
    convert_element_type x24 -> x21, other arithmetic: 11.8 us -> 5.07 us  [the longest x17 3.66 us: add(): (kept.astype(jnp.float32) + other.astype(jnp.float32)).astype(jnp.bfloat16)]
    dynamic_slice x25 -> x22, local copies, waits for them, and re-layouts: 6.04 us -> 1.72 us  [the longest x21 1.56 us: halves(): sent = lax.dynamic_slice_in_dim(part, (1 - mine) * width, width, axis)]
    dot_general x5, matrix products: 18.3 us -> 14.2 us  [dot_nn(): return jnp.dot(left, right, preferred_element_type=jnp.float32)]
    ppermute x12 -> x14, waiting for transfers between devices: 39.3 us -> 37.6 us  [swap_blocks(): return lax.ppermute(values, 'blk', [(0, 1), (1, 0)])]
    ppermute x12 -> x14, starting transfers between devices: 12.9 us -> 14.6 us  [swap_blocks(): return lax.ppermute(values, 'blk', [(0, 1), (1, 0)])]
  transfers between devices with their start and end apart: 48 -> 56, of which waited for: 29 -> 19; matrix products, arithmetic and copies ran while one was open for 13% -> 14% of each run, Pallas kernels for 14% -> 19%
where the time goes in v2:
time: 256 us; the launch traced here: 252 us
  waiting for transfers between devices  78.7 us (31%)
  starting transfers between devices  60.8 us (24%)
  Pallas kernels  48 us (19%)
  matrix products  33.1 us (13%)
  local copies, waits for them, and re-layouts  17 us (7%)
  other arithmetic  10.6 us (4%)
  between operations  3.51 us (1%)
    ppermute x42, starting transfers between devices, swap_items(): lax.ppermute(values, 'items', [(place, place ^ bit) for place in range(it...  46.1 us
    ppermute x42, waiting for transfers between devices, swap_items(): lax.ppermute(values, 'items', [(place, place ^ bit) for place in range(it...  41.1 us
    ppermute x14, waiting for transfers between devices, swap_blocks(): return lax.ppermute(values, 'blk', [(0, 1), (1, 0)])  37.6 us
    pallas_call x3, Pallas kernels, attend_back(): pl.pallas_call(attend_back_kernel, grid=(1, length // rows), in_specs=[pl...  30.4 us
    pallas_call x2, Pallas kernels, attend(): pl.pallas_call(attend_kernel, grid=(some, length // rows), in_specs=[pl.B...  17.6 us
    ppermute x14, starting transfers between devices, swap_blocks(): return lax.ppermute(values, 'blk', [(0, 1), (1, 0)])  14.6 us
    dot_general x5, matrix products, dot_nn(): return jnp.dot(left, right, preferred_element_type=jnp.float32)  14.2 us
    dot_general x5, matrix products, dot_tn(): lax.dot_general(left, right, (((0,), (0,)), ((), ())), preferred_element_...  10.3 us
  transfers between devices with their start and end apart: 56, of which 19 were waited for; matrix products, arithmetic and copies ran while one was open for 14% of the time, Pallas kernels for 19%

profile of v2, /device:TPU:0, one launch (start us, length us, event | category | flops | bytes accessed | tf_op | source)
XLA Modules:
  0.0 251.6 jit_solution(6076163317824570167)
XLA Ops:
  1.5 4.1 %collective-permute-start.1 = (bf16[1,1,1,1,48,1152]{5,4,3,2,1,0:T(8,128)(2,1)S(1)}, bf16[1,1,1,1,48,1152]{5,4,3,2,1,0:T(8,128)(2,1)S(1)}, u32[]{:S(2)}, u32[]{:S(2)}) collective-permute-start(bf16[1,1,1,1,48,1152]{5,4,3,2,1,0:T(8,128)(2,1)S(1)} %maximum_bitcast_fusion), channel_id=1, source_target_pairs={{0,16},{2,18},{4,20},{6,22},{8,24},{10,26},{12,28},{14,30},{16,0},... | collective-permute-start | bytes 331784 | tf_op jit(solution)/shard_map/ppermute | solution.py:254
  5.6 1.5 collective-permute-start.2
  7.4 2.6 %collective-permute-start.5 = (bf16[1,1,1,1,48,1024]{5,4,3,2,1,0:T(8,128)(2,1)}, bf16[1,1,1,1,48,1024]{5,4,3,2,1,0:T(8,128)(2,1)}, u32[]{:S(2)}, u32[]{:S(2)}) collective-permute-start(bf16[1,1,1,1,48,1024]{5,4,3,2,1,0:T(8,128)(2,1)} %bitcast.111), channel_id=1, source_target_pairs={{0,16},{2,18},{4,20},{6,22},{8,24},{10,26},{12,28},{14,30},{16,0},... | collective-permute-start | bytes 294920 | tf_op jit(solution)/shard_map/ppermute | solution.py:254
  16.9 1.2 collective-permute-start.3
  19.0 1.6 collective-permute-start.6
  21.5 3.2 %collective-permute-done.6 = bf16[1,1,1,1,128,768]{5,4,3,2,1,0:T(8,128)(2,1)S(1)} collective-permute-done((bf16[1,1,1,1,128,768]{5,4,3,2,1,0:T(8,128)(2,1)S(1)}, bf16[1,1,1,1,128,768]{5,4,3,2,1,0:T(8,128)(2,1)S(1)}, u32[]{:S(2)}, u32[]{:S(2)}) %collective-permute-start.6) | collective-permute-done | bytes 196640 | tf_op jit(solution)/shard_map/ppermute | solution.py:254
  24.8 1.0 collective-permute-done.3
  25.8 1.6 collective-permute-start.7
  29.3 2.0 collective-permute-start.9
  31.6 4.6 %collective-permute-done.8 = bf16[2,1,1,1,48,1024]{5,4,3,2,1,0:T(8,128)(2,1)S(1)} collective-permute-done((bf16[2,1,1,1,48,1024]{5,4,3,2,1,0:T(8,128)(2,1)S(1)}, bf16[2,1,1,1,48,1024]{5,4,3,2,1,0:T(8,128)(2,1)S(1)}, u32[]{:S(2)}, u32[]{:S(2)}) %collective-permute-start.8) | collective-permute-done | bytes 196640 | tf_op jit(solution)/shard_map/ppermute | solution.py:254
  36.2 3.0 %collective-permute-done.9 = bf16[2,1,1,1,48,1024]{5,4,3,2,1,0:T(8,128)(2,1)S(1)} collective-permute-done((bf16[2,1,1,1,48,1024]{5,4,3,2,1,0:T(8,128)(2,1)S(1)}, bf16[2,1,1,1,48,1024]{5,4,3,2,1,0:T(8,128)(2,1)S(1)}, u32[]{:S(2)}, u32[]{:S(2)}) %collective-permute-start.9) | collective-permute-done | bytes 196640 | tf_op jit(solution)/shard_map/ppermute | solution.py:254
  39.6 1.6 collective-permute-start.13
  42.9 1.1 collective-permute-done.12
  44.0 1.6 collective-permute-start.16
  45.6 2.3 collective-permute-start.15
  48.0 2.3 convolution_convert_fusion.q_ref.k_ref.v_ref
  50.3 11.8 %attend.2 = bf16[1024,256]{1,0:T(8,128)(2,1)S(1)} custom-call(s32[1]{0:T(128)} %bitcast.1.count_ref, bf16[1024,1152]{1,0:T(8,128)(2,1)S(1)} %convolution_convert_fusion.q_ref.k_ref.v_ref, bf16[1024,1152]{1,0:T(8,128)(2,1)S(1)} %convolution_convert_fusion.q_ref.k_ref.v_ref, bf16[1024,1152]{1,0:T(8,128)(2,1)S(1)} %convolution_convert_fusion.q_ref.k_ref.v_ref), custom_call_target="tpu_custom_call" | custom-call | flops 4294967296 | bytes 2097152 | tf_op jit(solution)/shard_map/attend/pallas_call | solution.py:361
  62.4 2.9 %collective-permute-done.15 = bf16[1,1,2,1,128,768]{5,4,3,2,1,0:T(8,128)(2,1)S(1)} collective-permute-done((bf16[1,1,2,1,128,768]{5,4,3,2,1,0:T(8,128)(2,1)S(1)}, bf16[1,1,2,1,128,768]{5,4,3,2,1,0:T(8,128)(2,1)S(1)}, u32[]{:S(2)}, u32[]{:S(2)}) %collective-permute-start.15) | collective-permute-done | bytes 393248 | tf_op jit(solution)/shard_map/ppermute | solution.py:254
  67.7 1.3 collective-permute-start.19
  69.0 5.8 %attend.3 = bf16[1024,128]{1,0:T(8,128)(2,1)S(1)} custom-call(s32[1]{0:T(128)} %bitcast.1.count_ref, bf16[1024,1152]{1,0:T(8,128)(2,1)S(1)} %convolution_convert_fusion.q_ref.k_ref.v_ref, bf16[1024,1152]{1,0:T(8,128)(2,1)S(1)} %convolution_convert_fusion.q_ref.k_ref.v_ref, bf16[1024,1152]{1,0:T(8,128)(2,1)S(1)} %convolution_convert_fusion.q_ref.k_ref.v_ref), custom_call_target="tpu_custom_call" | custom-call | flops 2147483648 | bytes 1048576 | tf_op jit(solution)/shard_map/attend/pallas_call | solution.py:361
  74.8 1.3 collective-permute-start.22
  77.9 18.1 %collective-permute-done.18 = bf16[512,128]{1,0:T(8,128)(2,1)S(1)} collective-permute-done((bf16[512,128]{1,0:T(8,128)(2,1)S(1)}, bf16[512,128]{1,0:T(8,128)(2,1)S(1)}, u32[]{:S(2)}, u32[]{:S(2)}) %collective-permute-start.18) | collective-permute-done | bytes 131104 | tf_op jit(solution)/shard_map/ppermute | solution.py:258
  99.5 5.5 %collective-permute-done.23 = bf16[2,2,2,1,48,768]{5,4,3,2,1,0:T(8,128)(2,1)S(1)} collective-permute-done((bf16[2,2,2,1,48,768]{5,4,3,2,1,0:T(8,128)(2,1)S(1)}, bf16[2,2,2,1,48,768]{5,4,3,2,1,0:T(8,128)(2,1)S(1)}, u32[]{:S(2)}, u32[]{:S(2)}) %collective-permute-start.23) | collective-permute-done | bytes 589856 | tf_op jit(solution)/shard_map/ppermute | solution.py:254
  107.4 1.8 fusion.21
  109.2 1.8 fusion.43
  111.3 6.5 %fusion.6 = (bf16[512,2048]{1,0:T(8,128)(2,1)S(1)}, bf16[512,2048]{1,0:T(8,128)(2,1)S(1)}, bf16[512,2048]{1,0:T(8,128)(2,1)}) fusion(f32[512,2048]{1,0:T(8,128)S(1)} %fusion.43, f32[2048,512]{0,1:T(8,128)S(1)} %fusion.21, bf16[512,768]{1,0:T(8,128)(2,1)S(1)} %multiply_convert_fusion.1, bf16[768,2048]{1,0:T(8,128)(2,1)S(1)} %bitcast.97), kind=kOutput, calls=%fused_computation.8 | convolution fusion | flops 1637875712 | bytes 18612224 | tf_op jit(solution)/shard_map/dot_general | solution.py:339
  117.8 3.4 %convolution_convert_fusion.3 = bf16[2048,768]{1,0:T(8,128)(2,1)S(1)} fusion(bf16[512,2048]{1,0:T(8,128)(2,1)} %get-tuple-element.199, bf16[1,512,768]{2,1,0:T(8,128)(2,1)S(1)} %copy-done.1), kind=kOutput, calls=%fused_computation.21 | convolution fusion | flops 1612185600 | bytes 6029312 | tf_op jit(solution)/shard_map/dot_general | solution.py:335
  121.6 1.8 fusion.44
  123.5 2.7 %fusion.18 = bf16[1,512,768]{2,1,0:T(8,128)(2,1)} fusion(f32[512,768]{1,0:T(8,128)S(1)} %get-tuple-element.246, bf16[512,2048]{1,0:T(8,128)(2,1)S(1)} %copy-done.6, bf16[2048,768]{1,0:T(8,128)(2,1)S(1)} %bitcast.100), kind=kOutput, calls=%fused_computation.54 | convolution fusion | flops 1611399168 | bytes 7602176 | tf_op jit(solution)/shard_map/dot_general | solution.py:339
  126.2 1.9 convolution_add_fusion
  130.2 1.8 convolution_convert_fusion.1
  132.0 1.8 convolution_convert_fusion.2
  133.9 1.3 collective-permute-start.28
  135.7 0.9 collective-permute-start.29
  138.5 6.8 %collective-permute-done.28 = bf16[512,384]{1,0:T(8,128)(2,1)S(1)} collective-permute-done((bf16[512,384]{1,0:T(8,128)(2,1)S(1)}, bf16[512,384]{1,0:T(8,128)(2,1)S(1)}, u32[]{:S(2)}, u32[]{:S(2)}) %collective-permute-start.28) | collective-permute-done | bytes 393248 | tf_op jit(solution)/shard_map/ppermute | solution.py:258
  145.4 10.1 %attend_back.3 = (bf16[1024,128]{1,0:T(8,128)(2,1)S(1)}, bf16[1024,128]{1,0:T(8,128)(2,1)S(1)}, bf16[1024,128]{1,0:T(8,128)(2,1)S(1)}) custom-call(s32[1]{0:T(128)} %bitcast.1.count_ref, bf16[1024,1152]{1,0:T(8,128)(2,1)S(1)} %convolution_convert_fusion.q_ref.k_ref.v_ref, bf16[1024,1152]{1,0:T(8,128)(2,1)S(1)} %convolution_convert_fusion.q_ref.k_ref.v_ref, ...), custom_call_target="tpu_custom_call" | custom-call | flops 5242880000 | bytes 1835008 | tf_op jit(solution)/shard_map/attend_back/pallas_call | solution.py:416
  155.7 1.1 collective-permute-start.37
  159.3 1.4 collective-permute-start.31
  161.0 3.5 %collective-permute-start.38 = (bf16[1,1,2,1,128,768]{5,4,3,2,1,0:T(8,128)(2,1)S(1)}, bf16[1,1,2,1,128,768]{5,4,3,2,1,0:T(8,128)(2,1)S(1)}, u32[]{:S(2)}, u32[]{:S(2)}) collective-permute-start(bf16[1,1,2,1,128,768]{5,4,3,2,1,0:T(8,128)(2,1)S(1)} %get-tuple-element.214), channel_id=1, source_target_pairs={{0,16},{2,18},{4,20},{6,22},{8,24},{10,26},{12,28},{14,30},{16,0},... | collective-permute-start | bytes 1179656 | tf_op jit(solution)/shard_map/ppermute | solution.py:254
  164.4 10.0 %attend_back.4 = (bf16[1024,128]{1,0:T(8,128)(2,1)S(1)}, bf16[1024,128]{1,0:T(8,128)(2,1)S(1)}, bf16[1024,128]{1,0:T(8,128)(2,1)S(1)}) custom-call(s32[1]{0:T(128)} %bitcast.1.count_ref, bf16[1024,1152]{1,0:T(8,128)(2,1)S(1)} %convolution_convert_fusion.q_ref.k_ref.v_ref, bf16[1024,1152]{1,0:T(8,128)(2,1)S(1)} %convolution_convert_fusion.q_ref.k_ref.v_ref, ...), custom_call_target="tpu_custom_call" | custom-call | flops 5242880000 | bytes 1835008 | tf_op jit(solution)/shard_map/attend_back/pallas_call | solution.py:416
  174.5 2.0 collective-permute-done.33
  176.4 4.6 %collective-permute-done.31 = bf16[2,2,1,1,48,2048]{5,4,3,2,1,0:T(8,128)(2,1)S(1)} collective-permute-done((bf16[2,2,1,1,48,2048]{5,4,3,2,1,0:T(8,128)(2,1)S(1)}, bf16[2,2,1,1,48,2048]{5,4,3,2,1,0:T(8,128)(2,1)S(1)}, u32[]{:S(2)}, u32[]{:S(2)}) %collective-permute-start.31) | collective-permute-done | bytes 786464 | tf_op jit(solution)/shard_map/ppermute | solution.py:254
  181.4 1.1 collective-permute-start.35
  183.8 10.2 %attend_back.5 = (bf16[1024,128]{1,0:T(8,128)(2,1)S(1)}, bf16[1024,128]{1,0:T(8,128)(2,1)S(1)}, bf16[1024,128]{1,0:T(8,128)(2,1)S(1)}) custom-call(s32[1]{0:T(128)} %bitcast.1.count_ref, bf16[1024,1152]{1,0:T(8,128)(2,1)S(1)} %convolution_convert_fusion.q_ref.k_ref.v_ref, bf16[1024,1152]{1,0:T(8,128)(2,1)S(1)} %convolution_convert_fusion.q_ref.k_ref.v_ref, ...), custom_call_target="tpu_custom_call" | custom-call | flops 5242880000 | bytes 1835008 | tf_op jit(solution)/shard_map/attend_back/pallas_call | solution.py:416
  194.8 2.4 convolution_convert_fusion.4
  197.2 2.3 fusion.11
  199.7 1.3 collective-permute-start.39
  201.4 1.8 collective-permute-start.44
  203.6 1.3 collective-permute-start.40
  205.2 1.2 collective-permute-start.43
  206.4 0.9 collective-permute-start.49
  207.4 1.2 collective-permute-start.45
  208.7 4.0 %collective-permute-done.44 = bf16[2,1,1,1,48,2048]{5,4,3,2,1,0:T(8,128)(2,1)S(1)} collective-permute-done((bf16[2,1,1,1,48,2048]{5,4,3,2,1,0:T(8,128)(2,1)S(1)}, bf16[2,1,1,1,48,2048]{5,4,3,2,1,0:T(8,128)(2,1)S(1)}, u32[]{:S(2)}, u32[]{:S(2)}) %collective-permute-start.44) | collective-permute-done | bytes 393248 | tf_op jit(solution)/shard_map/ppermute | solution.py:254
  213.5 10.5 %collective-permute-done.40 = bf16[512,768]{1,0:T(8,128)(2,1)S(1)} collective-permute-done((bf16[512,768]{1,0:T(8,128)(2,1)S(1)}, bf16[512,768]{1,0:T(8,128)(2,1)S(1)}, u32[]{:S(2)}, u32[]{:S(2)}) %collective-permute-start.40) | collective-permute-done | bytes 786464 | tf_op jit(solution)/shard_map/ppermute | solution.py:258
  224.2 3.5 %collective-permute-start.47 = (bf16[1,1,1,1,48,2048]{5,4,3,2,1,0:T(8,128)(2,1)S(1)}, bf16[1,1,1,1,48,2048]{5,4,3,2,1,0:T(8,128)(2,1)S(1)}, u32[]{:S(2)}, u32[]{:S(2)}) collective-permute-start(bf16[1,1,1,1,48,2048]{5,4,3,2,1,0:T(8,128)(2,1)S(1)} %get-tuple-element.232), channel_id=1, source_target_pairs={{0,16},{2,18},{4,20},{6,22},{8,24},{10,26},{12,28},{14,30},{16,0},... | collective-permute-start | bytes 589832 | tf_op jit(solution)/shard_map/ppermute | solution.py:254
  228.2 1.7 collective-permute-start.50
  230.4 1.5 fusion.19
  231.9 6.5 %collective-permute-done.50 = f32[2,768]{1,0:T(2,128)S(1)} collective-permute-done((f32[2,768]{1,0:T(2,128)S(1)}, f32[2,768]{1,0:T(2,128)S(1)}, u32[]{:S(2)}, u32[]{:S(2)}) %collective-permute-start.50) | collective-permute-done | bytes 6176 | tf_op jit(solution)/shard_map/ppermute | solution.py:254
  240.2 1.4 collective-permute-start.51
  241.6 1.6 collective-permute-start.52
  243.3 1.9 collective-permute-done.51
  245.8 1.3 collective-permute-start.54
  247.9 1.2 collective-permute-done.52
  249.8 1.0 collective-permute-done.54
  (241 shorter events, 41.1 us)
Async XLA Ops:
  0.6 13.3 %copy-start.2 = (bf16[128,384]{1,0:T(8,128)(2,1)S(1)}, bf16[128,384]{1,0:T(8,128)(2,1)}, u32[]{:S(2)}) copy-start(bf16[128,384]{1,0:T(8,128)(2,1)} %param.22) | copy-start | bytes 294916
  1.5 12.6 %copy-start = (bf16[1,512,768]{2,1,0:T(8,128)(2,1)S(1)}, bf16[1,512,768]{2,1,0:T(8,128)(2,1)}, u32[]{:S(2)}) copy-start(bf16[1,512,768]{2,1,0:T(8,128)(2,1)} %param.12) | copy-start | bytes 2359300
  1.5 15.4 %collective-permute-start.1 = (bf16[1,1,1,1,48,1152]{5,4,3,2,1,0:T(8,128)(2,1)S(1)}, bf16[1,1,1,1,48,1152]{5,4,3,2,1,0:T(8,128)(2,1)S(1)}, u32[]{:S(2)}, u32[]{:S(2)}) collective-permute-start(bf16[1,1,1,1,48,1152]{5,4,3,2,1,0:T(8,128)(2,1)S(1)} %maximum_bitcast_fusion), channel_id=1, source_target_pairs={{0,16},{2,18},{4,20},{6,22},{8,24},{10,26},{12,28},{14,30},{16,0},... | collective-permute-start | bytes 331784 | tf_op jit(solution)/shard_map/ppermute | solution.py:254
  5.6 10.8 %collective-permute-start.2 = (bf16[1,1,1,1,128,384]{5,4,3,2,1,0:T(8,128)(2,1)}, bf16[1,1,1,1,128,384]{5,4,3,2,1,0:T(8,128)(2,1)}, u32[]{:S(2)}, u32[]{:S(2)}) collective-permute-start(bf16[1,1,1,1,128,384]{5,4,3,2,1,0:T(8,128)(2,1)} %bitcast.109), channel_id=1, source_target_pairs={{0,1},{1,0},{2,3},{3,2},{4,5},{5,4},{6,7},{7,6},{8,9},{9,8},{10,11... | collective-permute-start | bytes 294920 | tf_op jit(solution)/shard_map/ppermute | solution.py:258
  7.1 13.6 %collective-permute-start.4 = (bf16[1,1,1,1,48,1024]{5,4,3,2,1,0:T(8,128)(2,1)}, bf16[1,1,1,1,48,1024]{5,4,3,2,1,0:T(8,128)(2,1)}, u32[]{:S(2)}, u32[]{:S(2)}) collective-permute-start(bf16[1,1,1,1,48,1024]{5,4,3,2,1,0:T(8,128)(2,1)} %bitcast.110), channel_id=1, source_target_pairs={{0,16},{2,18},{4,20},{6,22},{8,24},{10,26},{12,28},{14,30},{16,0},... | collective-permute-start | bytes 294920 | tf_op jit(solution)/shard_map/ppermute | solution.py:254
  7.4 14.1 %collective-permute-start.5 = (bf16[1,1,1,1,48,1024]{5,4,3,2,1,0:T(8,128)(2,1)}, bf16[1,1,1,1,48,1024]{5,4,3,2,1,0:T(8,128)(2,1)}, u32[]{:S(2)}, u32[]{:S(2)}) collective-permute-start(bf16[1,1,1,1,48,1024]{5,4,3,2,1,0:T(8,128)(2,1)} %bitcast.111), channel_id=1, source_target_pairs={{0,16},{2,18},{4,20},{6,22},{8,24},{10,26},{12,28},{14,30},{16,0},... | collective-permute-start | bytes 294920 | tf_op jit(solution)/shard_map/ppermute | solution.py:254
  10.0 21.6 %collective-permute-start.10 = (bf16[1,1,1,1,48,384]{5,4,3,2,1,0:T(8,128)(2,1)}, bf16[1,1,1,1,48,384]{5,4,3,2,1,0:T(8,128)(2,1)S(1)}, u32[]{:S(2)}, u32[]{:S(2)}) collective-permute-start(bf16[1,1,1,1,48,384]{5,4,3,2,1,0:T(8,128)(2,1)} %bitcast.112), channel_id=1, source_target_pairs={{0,16},{2,18},{4,20},{6,22},{8,24},{10,26},{12,28},{14,30},{16,0},... | collective-permute-start | bytes 110600 | tf_op jit(solution)/shard_map/ppermute | solution.py:254
  13.9 0.7 copy-start.5
  16.9 8.9 %collective-permute-start.3 = (bf16[2,1,1,1,48,1152]{5,4,3,2,1,0:T(8,128)(2,1)S(1)}, bf16[2,1,1,1,48,1152]{5,4,3,2,1,0:T(8,128)(2,1)S(1)}, u32[]{:S(2)}, u32[]{:S(2)}) collective-permute-start(bf16[2,1,1,1,48,1152]{5,4,3,2,1,0:T(8,128)(2,1)S(1)} %constant_dynamic-update-slice_fusion.47), channel_id=1, source_target_pairs={{0,8},{2,10},{4,12},{6,14},{8,0},{10,2},{12,4},{14,6},{16,24},{18,... | collective-permute-start | bytes 663560 | tf_op jit(solution)/shard_map/ppermute | solution.py:254
  19.0 5.7 %collective-permute-start.6 = (bf16[1,1,1,1,128,768]{5,4,3,2,1,0:T(8,128)(2,1)S(1)}, bf16[1,1,1,1,128,768]{5,4,3,2,1,0:T(8,128)(2,1)S(1)}, u32[]{:S(2)}, u32[]{:S(2)}) collective-permute-start(bf16[1,1,1,1,128,768]{5,4,3,2,1,0:T(8,128)(2,1)S(1)} %constant_dynamic-update-slice_fusion.44), channel_id=1, source_target_pairs={{0,4},{2,6},{4,0},{6,2},{8,12},{10,14},{12,8},{14,10},{16,20},{18,... | collective-permute-start | bytes 589832 | tf_op jit(solution)/shard_map/ppermute | solution.py:254
  20.8 21.6 %collective-permute-start = (bf16[512,768]{1,0:T(8,128)(2,1)S(1)}, bf16[512,768]{1,0:T(8,128)(2,1)S(1)}, u32[]{:S(2)}, u32[]{:S(2)}) collective-permute-start(bf16[512,768]{1,0:T(8,128)(2,1)S(1)} %bitcast.90), channel_id=1, source_target_pairs={{0,1},{1,0},{2,3},{3,2},{4,5},{5,4},{6,7},{7,6},{8,9},{9,8},{10,11... | collective-permute-start | bytes 2359304 | tf_op jit(solution)/shard_map/ppermute | solution.py:258
  25.8 13.3 %collective-permute-start.7 = (bf16[2,2,1,1,48,1152]{5,4,3,2,1,0:T(8,128)(2,1)S(1)}, bf16[2,2,1,1,48,1152]{5,4,3,2,1,0:T(8,128)(2,1)S(1)}, u32[]{:S(2)}, u32[]{:S(2)}) collective-permute-start(bf16[2,2,1,1,48,1152]{5,4,3,2,1,0:T(8,128)(2,1)S(1)} %constant_dynamic-update-slice_fusion.43), channel_id=1, source_target_pairs={{0,4},{2,6},{4,0},{6,2},{8,12},{10,14},{12,8},{14,10},{16,20},{18,... | collective-permute-start | bytes 1327112 | tf_op jit(solution)/shard_map/ppermute | solution.py:254
  28.4 7.8 %collective-permute-start.8 = (bf16[2,1,1,1,48,1024]{5,4,3,2,1,0:T(8,128)(2,1)S(1)}, bf16[2,1,1,1,48,1024]{5,4,3,2,1,0:T(8,128)(2,1)S(1)}, u32[]{:S(2)}, u32[]{:S(2)}) collective-permute-start(bf16[2,1,1,1,48,1024]{5,4,3,2,1,0:T(8,128)(2,1)S(1)} %constant_dynamic-update-slice_fusion.40), channel_id=1, source_target_pairs={{0,8},{2,10},{4,12},{6,14},{8,0},{10,2},{12,4},{14,6},{16,24},{18,... | collective-permute-start | bytes 589832 | tf_op jit(solution)/shard_map/ppermute | solution.py:254
  29.3 9.8 %collective-permute-start.9 = (bf16[2,1,1,1,48,1024]{5,4,3,2,1,0:T(8,128)(2,1)S(1)}, bf16[2,1,1,1,48,1024]{5,4,3,2,1,0:T(8,128)(2,1)S(1)}, u32[]{:S(2)}, u32[]{:S(2)}) collective-permute-start(bf16[2,1,1,1,48,1024]{5,4,3,2,1,0:T(8,128)(2,1)S(1)} %constant_dynamic-update-slice_fusion.38), channel_id=1, source_target_pairs={{0,8},{2,10},{4,12},{6,14},{8,0},{10,2},{12,4},{14,6},{16,24},{18,... | collective-permute-start | bytes 589832 | tf_op jit(solution)/shard_map/ppermute | solution.py:254
  39.2 4.8 %collective-permute-start.11 = (bf16[2,2,2,1,48,1152]{5,4,3,2,1,0:T(8,128)(2,1)S(1)}, bf16[2,2,2,1,48,1152]{5,4,3,2,1,0:T(8,128)(2,1)S(1)}, u32[]{:S(2)}, u32[]{:S(2)}) collective-permute-start(bf16[2,2,2,1,48,1152]{5,4,3,2,1,0:T(8,128)(2,1)S(1)} %constant_dynamic-update-slice_fusion.35), channel_id=1, source_target_pairs={{0,2},{2,0},{4,6},{6,4},{8,10},{10,8},{12,14},{14,12},{16,18},{18,... | collective-permute-start | bytes 2654216 | tf_op jit(solution)/shard_map/ppermute | solution.py:254
  39.3 4.7 %collective-permute-start.12 = (bf16[2,1,1,1,48,384]{5,4,3,2,1,0:T(8,128)(2,1)S(1)}, bf16[2,1,1,1,48,384]{5,4,3,2,1,0:T(8,128)(2,1)S(1)}, u32[]{:S(2)}, u32[]{:S(2)}) collective-permute-start(bf16[2,1,1,1,48,384]{5,4,3,2,1,0:T(8,128)(2,1)S(1)} %constant_dynamic-update-slice_fusion.32), channel_id=1, source_target_pairs={{0,8},{2,10},{4,12},{6,14},{8,0},{10,2},{12,4},{14,6},{16,24},{18,... | collective-permute-start | bytes 221192 | tf_op jit(solution)/shard_map/ppermute | solution.py:254
  39.6 22.7 %collective-permute-start.13 = (bf16[2,2,1,1,48,1024]{5,4,3,2,1,0:T(8,128)(2,1)S(1)}, bf16[2,2,1,1,48,1024]{5,4,3,2,1,0:T(8,128)(2,1)S(1)}, u32[]{:S(2)}, u32[]{:S(2)}) collective-permute-start(bf16[2,2,1,1,48,1024]{5,4,3,2,1,0:T(8,128)(2,1)S(1)} %constant_dynamic-update-slice_fusion.29), channel_id=1, source_target_pairs={{0,1},{1,0},{2,3},{3,2},{4,5},{5,4},{6,7},{7,6},{8,9},{9,8},{10,11... | collective-permute-start | bytes 1179656 | tf_op jit(solution)/shard_map/ppermute | solution.py:258
  41.2 21.2 %collective-permute-start.14 = (bf16[2,2,1,1,48,1024]{5,4,3,2,1,0:T(8,128)(2,1)S(1)}, bf16[2,2,1,1,48,1024]{5,4,3,2,1,0:T(8,128)(2,1)S(1)}, u32[]{:S(2)}, u32[]{:S(2)}) collective-permute-start(bf16[2,2,1,1,48,1024]{5,4,3,2,1,0:T(8,128)(2,1)S(1)} %constant_dynamic-update-slice_fusion.27), channel_id=1, source_target_pairs={{0,4},{2,6},{4,0},{6,2},{8,12},{10,14},{12,8},{14,10},{16,20},{18,... | collective-permute-start | bytes 1179656 | tf_op jit(solution)/shard_map/ppermute | solution.py:254
  42.5 5.5 %copy-start.4 = (f32[768]{0:T(1024)S(1)}, f32[768]{0:T(1024)}, u32[]{:S(2)}) copy-start(f32[768]{0:T(1024)} %param.14) | copy-start | bytes 9220
  44.0 18.4 %collective-permute-start.16 = (bf16[2,2,1,1,48,384]{5,4,3,2,1,0:T(8,128)(2,1)S(1)}, bf16[2,2,1,1,48,384]{5,4,3,2,1,0:T(8,128)(2,1)S(1)}, u32[]{:S(2)}, u32[]{:S(2)}) collective-permute-start(bf16[2,2,1,1,48,384]{5,4,3,2,1,0:T(8,128)(2,1)S(1)} %constant_dynamic-update-slice_fusion.25), channel_id=1, source_target_pairs={{0,1},{1,0},{2,3},{3,2},{4,5},{5,4},{6,7},{7,6},{8,9},{9,8},{10,11... | collective-permute-start | bytes 442376 | tf_op jit(solution)/shard_map/ppermute | solution.py:258
  45.6 19.8 %collective-permute-start.15 = (bf16[1,1,2,1,128,768]{5,4,3,2,1,0:T(8,128)(2,1)S(1)}, bf16[1,1,2,1,128,768]{5,4,3,2,1,0:T(8,128)(2,1)S(1)}, u32[]{:S(2)}, u32[]{:S(2)}) collective-permute-start(bf16[1,1,2,1,128,768]{5,4,3,2,1,0:T(8,128)(2,1)S(1)} %constant_dynamic-update-slice_fusion.36), channel_id=1, source_target_pairs={{0,16},{2,18},{4,20},{6,22},{8,24},{10,26},{12,28},{14,30},{16,0},... | collective-permute-start | bytes 1179656 | tf_op jit(solution)/shard_map/ppermute | solution.py:254
  65.4 9.4 %collective-permute-start.17 = (bf16[512,256]{1,0:T(8,128)(2,1)S(1)}, bf16[512,256]{1,0:T(8,128)(2,1)S(1)}, u32[]{:S(2)}, u32[]{:S(2)}) collective-permute-start(bf16[512,256]{1,0:T(8,128)(2,1)S(1)} %get-tuple-element.224), channel_id=1, source_target_pairs={{0,1},{1,0},{2,3},{3,2},{4,5},{5,4},{6,7},{7,6},{8,9},{9,8},{10,11... | collective-permute-start | bytes 786440 | tf_op jit(solution)/shard_map/ppermute | solution.py:258
  66.0 30.0 %collective-permute-start.21 = (bf16[2,1,2,1,128,768]{5,4,3,2,1,0:T(8,128)(2,1)S(1)}, bf16[2,1,2,1,128,768]{5,4,3,2,1,0:T(8,128)(2,1)S(1)}, u32[]{:S(2)}, u32[]{:S(2)}) collective-permute-start(bf16[2,1,2,1,128,768]{5,4,3,2,1,0:T(8,128)(2,1)S(1)} %constant_dynamic-update-slice_fusion.17), channel_id=1, source_target_pairs={{0,8},{2,10},{4,12},{6,14},{8,0},{10,2},{12,4},{14,6},{16,24},{18,... | collective-permute-start | bytes 2359304 | tf_op jit(solution)/shard_map/ppermute | solution.py:254
  66.8 29.2 %collective-permute-start.20 = (bf16[2,2,1,1,48,2048]{5,4,3,2,1,0:T(8,128)(2,1)S(1)}, bf16[2,2,1,1,48,2048]{5,4,3,2,1,0:T(8,128)(2,1)S(1)}, u32[]{:S(2)}, u32[]{:S(2)}) collective-permute-start(bf16[2,2,1,1,48,2048]{5,4,3,2,1,0:T(8,128)(2,1)S(1)} %constant_dynamic-update-slice_fusion.19), channel_id=1, source_target_pairs={{0,4},{2,6},{4,0},{6,2},{8,12},{10,14},{12,8},{14,10},{16,20},{18,... | collective-permute-start | bytes 2359304 | tf_op jit(solution)/shard_map/ppermute | solution.py:254
  67.7 28.3 %collective-permute-start.19 = (bf16[2,2,1,1,48,768]{5,4,3,2,1,0:T(8,128)(2,1)S(1)}, bf16[2,2,1,1,48,768]{5,4,3,2,1,0:T(8,128)(2,1)S(1)}, u32[]{:S(2)}, u32[]{:S(2)}) collective-permute-start(bf16[2,2,1,1,48,768]{5,4,3,2,1,0:T(8,128)(2,1)S(1)} %constant_dynamic-update-slice_fusion.21), channel_id=1, source_target_pairs={{0,4},{2,6},{4,0},{6,2},{8,12},{10,14},{12,8},{14,10},{16,20},{18,... | collective-permute-start | bytes 884744 | tf_op jit(solution)/shard_map/ppermute | solution.py:254
  74.8 21.2 %collective-permute-start.22 = (bf16[2,2,2,1,48,1024]{5,4,3,2,1,0:T(8,128)(2,1)S(1)}, bf16[2,2,2,1,48,1024]{5,4,3,2,1,0:T(8,128)(2,1)S(1)}, u32[]{:S(2)}, u32[]{:S(2)}) collective-permute-start(bf16[2,2,2,1,48,1024]{5,4,3,2,1,0:T(8,128)(2,1)S(1)} %constant_dynamic-update-slice_fusion.23), channel_id=1, source_target_pairs={{0,1},{1,0},{2,3},{3,2},{4,5},{5,4},{6,7},{7,6},{8,9},{9,8},{10,11... | collective-permute-start | bytes 2359304 | tf_op jit(solution)/shard_map/ppermute | solution.py:258
  76.1 19.9 %collective-permute-start.18 = (bf16[512,128]{1,0:T(8,128)(2,1)S(1)}, bf16[512,128]{1,0:T(8,128)(2,1)S(1)}, u32[]{:S(2)}, u32[]{:S(2)}) collective-permute-start(bf16[512,128]{1,0:T(8,128)(2,1)S(1)} %get-tuple-element.236), channel_id=1, source_target_pairs={{0,1},{1,0},{2,3},{3,2},{4,5},{5,4},{6,7},{7,6},{8,9},{9,8},{10,11... | collective-permute-start | bytes 393224 | tf_op jit(solution)/shard_map/ppermute | solution.py:258
  96.1 15.0 %collective-permute-start.24 = (bf16[2,2,2,1,48,2048]{5,4,3,2,1,0:T(8,128)(2,1)S(1)}, bf16[2,2,2,1,48,2048]{5,4,3,2,1,0:T(8,128)(2,1)S(1)}, u32[]{:S(2)}, u32[]{:S(2)}) collective-permute-start(bf16[2,2,2,1,48,2048]{5,4,3,2,1,0:T(8,128)(2,1)S(1)} %constant_dynamic-update-slice_fusion.11), channel_id=1, source_target_pairs={{0,2},{2,0},{4,6},{6,4},{8,10},{10,8},{12,14},{14,12},{16,18},{18,... | collective-permute-start | bytes 4718600 | tf_op jit(solution)/shard_map/ppermute | solution.py:254
  96.9 9.2 %collective-permute-start.26 = (bf16[2,2,2,1,128,768]{5,4,3,2,1,0:T(8,128)(2,1)S(1)}, bf16[2,2,2,1,128,768]{5,4,3,2,1,0:T(8,128)(2,1)S(1)}, u32[]{:S(2)}, u32[]{:S(2)}) collective-permute-start(bf16[2,2,2,1,128,768]{5,4,3,2,1,0:T(8,128)(2,1)S(1)} %constant_dynamic-update-slice_fusion.3), channel_id=1, source_target_pairs={{0,2},{2,0},{4,6},{6,4},{8,10},{10,8},{12,14},{14,12},{16,18},{18,... | collective-permute-start | bytes 4718600 | tf_op jit(solution)/shard_map/ppermute | solution.py:254
  97.5 8.8 %collective-permute-start.25 = (bf16[2,2,2,1,48,2048]{5,4,3,2,1,0:T(8,128)(2,1)S(1)}, bf16[2,2,2,1,48,2048]{5,4,3,2,1,0:T(8,128)(2,1)S(1)}, u32[]{:S(2)}, u32[]{:S(2)}) collective-permute-start(bf16[2,2,2,1,48,2048]{5,4,3,2,1,0:T(8,128)(2,1)S(1)} %constant_dynamic-update-slice_fusion.7), channel_id=1, source_target_pairs={{0,2},{2,0},{4,6},{6,4},{8,10},{10,8},{12,14},{14,12},{16,18},{18,... | collective-permute-start | bytes 4718600 | tf_op jit(solution)/shard_map/ppermute | solution.py:254
  97.6 7.3 %collective-permute-start.23 = (bf16[2,2,2,1,48,768]{5,4,3,2,1,0:T(8,128)(2,1)S(1)}, bf16[2,2,2,1,48,768]{5,4,3,2,1,0:T(8,128)(2,1)S(1)}, u32[]{:S(2)}, u32[]{:S(2)}) collective-permute-start(bf16[2,2,2,1,48,768]{5,4,3,2,1,0:T(8,128)(2,1)S(1)} %constant_dynamic-update-slice_fusion.15), channel_id=1, source_target_pairs={{0,2},{2,0},{4,6},{6,4},{8,10},{10,8},{12,14},{14,12},{16,18},{18,... | collective-permute-start | bytes 1769480 | tf_op jit(solution)/shard_map/ppermute | solution.py:254
  105.0 0.9 copy-start.3
  106.3 1.1 copy-start.1
  121.4 6.6 %collective-permute-start.27 = (bf16[2,2,2,1,128,768]{5,4,3,2,1,0:T(8,128)(2,1)S(1)}, bf16[2,2,2,1,128,768]{5,4,3,2,1,0:T(8,128)(2,1)S(1)}, u32[]{:S(2)}, u32[]{:S(2)}) collective-permute-start(bf16[2,2,2,1,128,768]{5,4,3,2,1,0:T(8,128)(2,1)S(1)} %get-tuple-element.200), channel_id=1, source_target_pairs={{0,2},{2,0},{4,6},{6,4},{8,10},{10,8},{12,14},{14,12},{16,18},{18,... | collective-permute-start | bytes 4718600 | tf_op jit(solution)/shard_map/ppermute | solution.py:254
  121.6 1.8 copy-start.6
  133.9 11.4 %collective-permute-start.28 = (bf16[512,384]{1,0:T(8,128)(2,1)S(1)}, bf16[512,384]{1,0:T(8,128)(2,1)S(1)}, u32[]{:S(2)}, u32[]{:S(2)}) collective-permute-start(bf16[512,384]{1,0:T(8,128)(2,1)S(1)} %get-tuple-element.220), channel_id=1, source_target_pairs={{0,1},{1,0},{2,3},{3,2},{4,5},{5,4},{6,7},{7,6},{8,9},{9,8},{10,11... | collective-permute-start | bytes 1179656 | tf_op jit(solution)/shard_map/ppermute | solution.py:258
  135.7 21.1 %collective-permute-start.29 = (bf16[2,1,2,1,128,768]{5,4,3,2,1,0:T(8,128)(2,1)S(1)}, bf16[2,1,2,1,128,768]{5,4,3,2,1,0:T(8,128)(2,1)S(1)}, u32[]{:S(2)}, u32[]{:S(2)}) collective-permute-start(bf16[2,1,2,1,128,768]{5,4,3,2,1,0:T(8,128)(2,1)S(1)} %get-tuple-element.208), channel_id=1, source_target_pairs={{0,8},{2,10},{4,12},{6,14},{8,0},{10,2},{12,4},{14,6},{16,24},{18,... | collective-permute-start | bytes 2359304 | tf_op jit(solution)/shard_map/ppermute | solution.py:254
  136.8 20.1 %collective-permute-start.32 = (bf16[2,2,2,1,48,2048]{5,4,3,2,1,0:T(8,128)(2,1)S(1)}, bf16[2,2,2,1,48,2048]{5,4,3,2,1,0:T(8,128)(2,1)S(1)}, u32[]{:S(2)}, u32[]{:S(2)}) collective-permute-start(bf16[2,2,2,1,48,2048]{5,4,3,2,1,0:T(8,128)(2,1)S(1)} %constant_dynamic-slice_fusion.27), channel_id=1, source_target_pairs={{0,2},{2,0},{4,6},{6,4},{8,10},{10,8},{12,14},{14,12},{16,18},{18,... | collective-permute-start | bytes 4718600 | tf_op jit(solution)/shard_map/ppermute | solution.py:254
  137.7 17.7 %collective-permute-start.36 = (bf16[2,2,2,1,48,768]{5,4,3,2,1,0:T(8,128)(2,1)S(1)}, bf16[2,2,2,1,48,768]{5,4,3,2,1,0:T(8,128)(2,1)S(1)}, u32[]{:S(2)}, u32[]{:S(2)}) collective-permute-start(bf16[2,2,2,1,48,768]{5,4,3,2,1,0:T(8,128)(2,1)S(1)} %constant_dynamic-slice_fusion.20), channel_id=1, source_target_pairs={{0,2},{2,0},{4,6},{6,4},{8,10},{10,8},{12,14},{14,12},{16,18},{18,... | collective-permute-start | bytes 1769480 | tf_op jit(solution)/shard_map/ppermute | solution.py:254
  138.4 20.2 %collective-permute-start.30 = (bf16[2,2,2,1,48,2048]{5,4,3,2,1,0:T(8,128)(2,1)S(1)}, bf16[2,2,2,1,48,2048]{5,4,3,2,1,0:T(8,128)(2,1)S(1)}, u32[]{:S(2)}, u32[]{:S(2)}) collective-permute-start(bf16[2,2,2,1,48,2048]{5,4,3,2,1,0:T(8,128)(2,1)S(1)} %constant_dynamic-slice_fusion.30), channel_id=1, source_target_pairs={{0,2},{2,0},{4,6},{6,4},{8,10},{10,8},{12,14},{14,12},{16,18},{18,... | collective-permute-start | bytes 4718600 | tf_op jit(solution)/shard_map/ppermute | solution.py:254
  155.7 38.5 %collective-permute-start.37 = (bf16[2,2,1,1,48,768]{5,4,3,2,1,0:T(8,128)(2,1)S(1)}, bf16[2,2,1,1,48,768]{5,4,3,2,1,0:T(8,128)(2,1)S(1)}, u32[]{:S(2)}, u32[]{:S(2)}) collective-permute-start(bf16[2,2,1,1,48,768]{5,4,3,2,1,0:T(8,128)(2,1)S(1)} %get-tuple-element.222), channel_id=1, source_target_pairs={{0,4},{2,6},{4,0},{6,2},{8,12},{10,14},{12,8},{14,10},{16,20},{18,... | collective-permute-start | bytes 884744 | tf_op jit(solution)/shard_map/ppermute | solution.py:254
  157.7 18.8 %collective-permute-start.33 = (bf16[2,2,2,1,48,1024]{5,4,3,2,1,0:T(8,128)(2,1)S(1)}, bf16[2,2,2,1,48,1024]{5,4,3,2,1,0:T(8,128)(2,1)S(1)}, u32[]{:S(2)}, u32[]{:S(2)}) collective-permute-start(bf16[2,2,2,1,48,1024]{5,4,3,2,1,0:T(8,128)(2,1)S(1)} %get-tuple-element.204), channel_id=1, source_target_pairs={{0,1},{1,0},{2,3},{3,2},{4,5},{5,4},{6,7},{7,6},{8,9},{9,8},{10,11... | collective-permute-start | bytes 2359304 | tf_op jit(solution)/shard_map/ppermute | solution.py:258
  159.3 21.7 %collective-permute-start.31 = (bf16[2,2,1,1,48,2048]{5,4,3,2,1,0:T(8,128)(2,1)S(1)}, bf16[2,2,1,1,48,2048]{5,4,3,2,1,0:T(8,128)(2,1)S(1)}, u32[]{:S(2)}, u32[]{:S(2)}) collective-permute-start(bf16[2,2,1,1,48,2048]{5,4,3,2,1,0:T(8,128)(2,1)S(1)} %get-tuple-element.206), channel_id=1, source_target_pairs={{0,4},{2,6},{4,0},{6,2},{8,12},{10,14},{12,8},{14,10},{16,20},{18,... | collective-permute-start | bytes 2359304 | tf_op jit(solution)/shard_map/ppermute | solution.py:254
  161.0 33.3 %collective-permute-start.38 = (bf16[1,1,2,1,128,768]{5,4,3,2,1,0:T(8,128)(2,1)S(1)}, bf16[1,1,2,1,128,768]{5,4,3,2,1,0:T(8,128)(2,1)S(1)}, u32[]{:S(2)}, u32[]{:S(2)}) collective-permute-start(bf16[1,1,2,1,128,768]{5,4,3,2,1,0:T(8,128)(2,1)S(1)} %get-tuple-element.214), channel_id=1, source_target_pairs={{0,16},{2,18},{4,20},{6,22},{8,24},{10,26},{12,28},{14,30},{16,0},... | collective-permute-start | bytes 1179656 | tf_op jit(solution)/shard_map/ppermute | solution.py:254
  181.4 12.8 %collective-permute-start.35 = (bf16[2,2,1,1,48,1024]{5,4,3,2,1,0:T(8,128)(2,1)S(1)}, bf16[2,2,1,1,48,1024]{5,4,3,2,1,0:T(8,128)(2,1)S(1)}, u32[]{:S(2)}, u32[]{:S(2)}) collective-permute-start(bf16[2,2,1,1,48,1024]{5,4,3,2,1,0:T(8,128)(2,1)S(1)} %get-tuple-element.216), channel_id=1, source_target_pairs={{0,4},{2,6},{4,0},{6,2},{8,12},{10,14},{12,8},{14,10},{16,20},{18,... | collective-permute-start | bytes 1179656 | tf_op jit(solution)/shard_map/ppermute | solution.py:254
  182.9 11.3 %collective-permute-start.34 = (bf16[2,2,1,1,48,1024]{5,4,3,2,1,0:T(8,128)(2,1)S(1)}, bf16[2,2,1,1,48,1024]{5,4,3,2,1,0:T(8,128)(2,1)S(1)}, u32[]{:S(2)}, u32[]{:S(2)}) collective-permute-start(bf16[2,2,1,1,48,1024]{5,4,3,2,1,0:T(8,128)(2,1)S(1)} %get-tuple-element.218), channel_id=1, source_target_pairs={{0,1},{1,0},{2,3},{3,2},{4,5},{5,4},{6,7},{7,6},{8,9},{9,8},{10,11... | collective-permute-start | bytes 1179656 | tf_op jit(solution)/shard_map/ppermute | solution.py:258
  199.6 5.3 %collective-permute-start.41 = (bf16[2,2,2,1,48,1152]{5,4,3,2,1,0:T(8,128)(2,1)S(1)}, bf16[2,2,2,1,48,1152]{5,4,3,2,1,0:T(8,128)(2,1)S(1)}, u32[]{:S(2)}, u32[]{:S(2)}) collective-permute-start(bf16[2,2,2,1,48,1152]{5,4,3,2,1,0:T(8,128)(2,1)S(1)} %get-tuple-element.202), channel_id=1, source_target_pairs={{0,2},{2,0},{4,6},{6,4},{8,10},{10,8},{12,14},{14,12},{16,18},{18,... | collective-permute-start | bytes 2654216 | tf_op jit(solution)/shard_map/ppermute | solution.py:254
  199.7 3.7 %collective-permute-start.39 = (f32[2,768]{1,0:T(2,128)S(1)}, f32[2,768]{1,0:T(2,128)S(1)}, u32[]{:S(2)}, u32[]{:S(2)}) collective-permute-start(f32[2,768]{1,0:T(2,128)S(1)} %pad_maximum_fusion), channel_id=1, source_target_pairs={{0,1},{1,0},{2,3},{3,2},{4,5},{5,4},{6,7},{7,6},{8,9},{9,8},{10,11... | collective-permute-start | bytes 18440 | tf_op jit(solution)/shard_map/ppermute | solution.py:258
  201.4 11.3 %collective-permute-start.44 = (bf16[2,1,1,1,48,2048]{5,4,3,2,1,0:T(8,128)(2,1)S(1)}, bf16[2,1,1,1,48,2048]{5,4,3,2,1,0:T(8,128)(2,1)S(1)}, u32[]{:S(2)}, u32[]{:S(2)}) collective-permute-start(bf16[2,1,1,1,48,2048]{5,4,3,2,1,0:T(8,128)(2,1)S(1)} %get-tuple-element.212), channel_id=1, source_target_pairs={{0,8},{2,10},{4,12},{6,14},{8,0},{10,2},{12,4},{14,6},{16,24},{18,... | collective-permute-start | bytes 1179656 | tf_op jit(solution)/shard_map/ppermute | solution.py:254
  203.4 1.4 collective-permute-start.42
  203.6 20.4 %collective-permute-start.40 = (bf16[512,768]{1,0:T(8,128)(2,1)S(1)}, bf16[512,768]{1,0:T(8,128)(2,1)S(1)}, u32[]{:S(2)}, u32[]{:S(2)}) collective-permute-start(bf16[512,768]{1,0:T(8,128)(2,1)S(1)} %dynamic-slice_convert_fusion), channel_id=1, source_target_pairs={{0,1},{1,0},{2,3},{3,2},{4,5},{5,4},{6,7},{7,6},{8,9},{9,8},{10,11... | collective-permute-start | bytes 2359304 | tf_op jit(solution)/shard_map/ppermute | solution.py:258
  205.2 18.9 %collective-permute-start.43 = (bf16[2,2,1,1,48,1152]{5,4,3,2,1,0:T(8,128)(2,1)S(1)}, bf16[2,2,1,1,48,1152]{5,4,3,2,1,0:T(8,128)(2,1)S(1)}, u32[]{:S(2)}, u32[]{:S(2)}) collective-permute-start(bf16[2,2,1,1,48,1152]{5,4,3,2,1,0:T(8,128)(2,1)S(1)} %get-tuple-element.210), channel_id=1, source_target_pairs={{0,4},{2,6},{4,0},{6,2},{8,12},{10,14},{12,8},{14,10},{16,20},{18,... | collective-permute-start | bytes 1327112 | tf_op jit(solution)/shard_map/ppermute | solution.py:254
  206.4 25.5 %collective-permute-start.49 = (bf16[1,1,1,1,128,768]{5,4,3,2,1,0:T(8,128)(2,1)S(1)}, bf16[1,1,1,1,128,768]{5,4,3,2,1,0:T(8,128)(2,1)S(1)}, u32[]{:S(2)}, u32[]{:S(2)}) collective-permute-start(bf16[1,1,1,1,128,768]{5,4,3,2,1,0:T(8,128)(2,1)S(1)} %get-tuple-element.230), channel_id=1, source_target_pairs={{0,4},{2,6},{4,0},{6,2},{8,12},{10,14},{12,8},{14,10},{16,20},{18,... | collective-permute-start | bytes 589832 | tf_op jit(solution)/shard_map/ppermute | solution.py:254
  207.4 16.6 %collective-permute-start.45 = (f32[2,768]{1,0:T(2,128)S(1)}, f32[2,768]{1,0:T(2,128)S(1)}, u32[]{:S(2)}, u32[]{:S(2)}) collective-permute-start(f32[2,768]{1,0:T(2,128)S(1)} %add.309), channel_id=1, source_target_pairs={{0,4},{2,6},{4,0},{6,2},{8,12},{10,14},{12,8},{14,10},{16,20},{18,... | collective-permute-start | bytes 18440 | tf_op jit(solution)/shard_map/ppermute | solution.py:254
  212.7 19.2 %collective-permute-start.48 = (bf16[2,2,1,1,48,384]{5,4,3,2,1,0:T(8,128)(2,1)S(1)}, bf16[2,2,1,1,48,384]{5,4,3,2,1,0:T(8,128)(2,1)S(1)}, u32[]{:S(2)}, u32[]{:S(2)}) collective-permute-start(bf16[2,2,1,1,48,384]{5,4,3,2,1,0:T(8,128)(2,1)S(1)} %get-tuple-element.234), channel_id=1, source_target_pairs={{0,1},{1,0},{2,3},{3,2},{4,5},{5,4},{6,7},{7,6},{8,9},{9,8},{10,11... | collective-permute-start | bytes 442376 | tf_op jit(solution)/shard_map/ppermute | solution.py:258
  224.2 14.3 %collective-permute-start.47 = (bf16[1,1,1,1,48,2048]{5,4,3,2,1,0:T(8,128)(2,1)S(1)}, bf16[1,1,1,1,48,2048]{5,4,3,2,1,0:T(8,128)(2,1)S(1)}, u32[]{:S(2)}, u32[]{:S(2)}) collective-permute-start(bf16[1,1,1,1,48,2048]{5,4,3,2,1,0:T(8,128)(2,1)S(1)} %get-tuple-element.232), channel_id=1, source_target_pairs={{0,16},{2,18},{4,20},{6,22},{8,24},{10,26},{12,28},{14,30},{16,0},... | collective-permute-start | bytes 589832 | tf_op jit(solution)/shard_map/ppermute | solution.py:254
  227.8 10.7 %collective-permute-start.46 = (bf16[2,1,1,1,48,1152]{5,4,3,2,1,0:T(8,128)(2,1)S(1)}, bf16[2,1,1,1,48,1152]{5,4,3,2,1,0:T(8,128)(2,1)S(1)}, u32[]{:S(2)}, u32[]{:S(2)}) collective-permute-start(bf16[2,1,1,1,48,1152]{5,4,3,2,1,0:T(8,128)(2,1)S(1)} %get-tuple-element.226), channel_id=1, source_target_pairs={{0,8},{2,10},{4,12},{6,14},{8,0},{10,2},{12,4},{14,6},{16,24},{18,... | collective-permute-start | bytes 663560 | tf_op jit(solution)/shard_map/ppermute | solution.py:254
  228.2 10.3 %collective-permute-start.50 = (f32[2,768]{1,0:T(2,128)S(1)}, f32[2,768]{1,0:T(2,128)S(1)}, u32[]{:S(2)}, u32[]{:S(2)}) collective-permute-start(f32[2,768]{1,0:T(2,128)S(1)} %add.313), channel_id=1, source_target_pairs={{0,8},{2,10},{4,12},{6,14},{8,0},{10,2},{12,4},{14,6},{16,24},{18,... | collective-permute-start | bytes 18440 | tf_op jit(solution)/shard_map/ppermute | solution.py:254
  238.5 8.6 %collective-permute-start.55 = (bf16[1,1,1,1,128,384]{5,4,3,2,1,0:T(8,128)(2,1)S(1)}, bf16[1,1,1,1,128,384]{5,4,3,2,1,0:T(8,128)(2,1)S(1)}, u32[]{:S(2)}, u32[]{:S(2)}) collective-permute-start(bf16[1,1,1,1,128,384]{5,4,3,2,1,0:T(8,128)(2,1)S(1)} %constant_dynamic-slice_fusion), channel_id=1, source_target_pairs={{0,1},{1,0},{2,3},{3,2},{4,5},{5,4},{6,7},{7,6},{8,9},{9,8},{10,11... | collective-permute-start | bytes 294920 | tf_op jit(solution)/shard_map/ppermute | solution.py:258
  239.5 6.3 %collective-permute-start.53 = (bf16[2,1,1,1,48,384]{5,4,3,2,1,0:T(8,128)(2,1)S(1)}, bf16[2,1,1,1,48,384]{5,4,3,2,1,0:T(8,128)(2,1)S(1)}, u32[]{:S(2)}, u32[]{:S(2)}) collective-permute-start(bf16[2,1,1,1,48,384]{5,4,3,2,1,0:T(8,128)(2,1)S(1)} %constant_dynamic-slice_fusion.2), channel_id=1, source_target_pairs={{0,8},{2,10},{4,12},{6,14},{8,0},{10,2},{12,4},{14,6},{16,24},{18,... | collective-permute-start | bytes 221192 | tf_op jit(solution)/shard_map/ppermute | solution.py:254
  240.2 5.0 %collective-permute-start.51 = (f32[2,768]{1,0:T(2,128)S(1)}, f32[2,768]{1,0:T(2,128)S(1)}, u32[]{:S(2)}, u32[]{:S(2)}) collective-permute-start(f32[2,768]{1,0:T(2,128)S(1)} %add.318), channel_id=1, source_target_pairs={{0,16},{2,18},{4,20},{6,22},{8,24},{10,26},{12,28},{14,30},{16,0},... | collective-permute-start | bytes 18440 | tf_op jit(solution)/shard_map/ppermute | solution.py:254
  241.6 7.4 %collective-permute-start.52 = (bf16[1,1,1,1,48,1152]{5,4,3,2,1,0:T(8,128)(2,1)S(1)}, bf16[1,1,1,1,48,1152]{5,4,3,2,1,0:T(8,128)(2,1)S(1)}, u32[]{:S(2)}, u32[]{:S(2)}) collective-permute-start(bf16[1,1,1,1,48,1152]{5,4,3,2,1,0:T(8,128)(2,1)S(1)} %constant_dynamic-slice_fusion.3), channel_id=1, source_target_pairs={{0,16},{2,18},{4,20},{6,22},{8,24},{10,26},{12,28},{14,30},{16,0},... | collective-permute-start | bytes 331784 | tf_op jit(solution)/shard_map/ppermute | solution.py:254
  245.8 4.9 %collective-permute-start.54 = (bf16[1,1,1,1,48,384]{5,4,3,2,1,0:T(8,128)(2,1)S(1)}, bf16[1,1,1,1,48,384]{5,4,3,2,1,0:T(8,128)(2,1)S(1)}, u32[]{:S(2)}, u32[]{:S(2)}) collective-permute-start(bf16[1,1,1,1,48,384]{5,4,3,2,1,0:T(8,128)(2,1)S(1)} %constant_dynamic-slice_fusion.1), channel_id=1, source_target_pairs={{0,16},{2,18},{4,20},{6,22},{8,24},{10,26},{12,28},{14,30},{16,0},... | collective-permute-start | bytes 110600 | tf_op jit(solution)/shard_map/ppermute | solution.py:254
